TPU v7x, 256 devices: a whole 4x4x8 slice. The times are simulated.
256 devices in a mesh: tier: 4 (over y_hi, core), grp: 64 (over y_lo, z, x).
Axes of the slice: x: 4, y: 4 (y_hi: 2, y_lo: 2; y = y_hi * 2 + y_lo), z: 8, core: 2. Of those that a mesh axis runs over, the one named last changes fastest.
Arguments:
- resid: bfloat16 [256, 8192], P(('tier', 'grp')), may hold values from -1.5 to 1.5
- query: bfloat16 [256, 8192], P('tier', 'grp'), may hold values from -9 to 9
- fresh_kv: bfloat16 [256, 2048], P('tier', 'grp'), may hold values from -9 to 9
- cache_home: int32 [4, 64], P('tier'), may hold values from 0 to 63, each once within a row
- kv_cache: bfloat16 [256, 128, 2048], P(('tier', 'grp')), may hold values from -9 to 9
- cached_len: int32 [256], P(('tier', 'grp')), may hold values from 1 to 128, 16384 in all
- wo: bfloat16 [8192, 8192], P('grp'), may hold values from -0.0625 to 0.0625
- norm_gain: bfloat16 [8192], replicated, may hold values from 0.099609375 to 1.8984375
- w_router: bfloat16 [8192, 4], replicated, may hold values from -0.0625 to 0.0625
- expert_ids: int32 [256, 2], P(('tier', 'grp')), may hold values from 0 to 3, all different within a row; in each aligned block of 64 rows (0 to 63, 64 to 127, ...) at most 48 rows name the same one
- w_gate: bfloat16 [4, 12288, 8192], P('tier', 'grp'), may hold values from -0.0625 to 0.0625
- w_up: bfloat16 [4, 12288, 8192], P('tier', 'grp'), may hold values from -0.0625 to 0.0625
- w_down: bfloat16 [4, 12288, 8192], P('tier', 'grp'), may hold values from -0.0546875 to 0.0546875
Outputs:
- layer_out: bfloat16 [256, 8192], P(('tier', 'grp'))
Inputs may be any that keep to these rules, and one draw needn't show every extreme that they name: Each row of cache_home is a permutation of 0 .. 63. `expert_ids`: the two experts of a row differ; within the rows of one micro-batch (aligned blocks of 64 rows) no expert is named by more than 48 rows, a bound that some block reaches.
All inputs are finite; a program needn't handle non-finite values. No bound on the sum of `cached_len` on one device may be relied on, other than what follows from the above.
Results may differ from a plain program's by a relative error of at most 0.017.
Values may be sent and summed in bfloat16 or wider, within the bound.
A program may use at most 128 MiB of HBM per device.

v0:
```python
import math

import jax
import jax.numpy as jnp
from jax import lax
from jax.sharding import PartitionSpec as P

H = 64
G = 8
HD = 128
CTX = 128


def attend(my_query, my_fresh, kv_cache, cached_len):
    row_count = my_query.shape[0]
    per_kv = H // G
    queries = my_query.reshape(row_count, G, per_kv, HD)
    cached_keys = kv_cache[:, :, : G * HD].reshape(row_count, CTX, G, HD)
    cached_values = kv_cache[:, :, G * HD :].reshape(row_count, CTX, G, HD)
    new_key = my_fresh[:, : G * HD].reshape(row_count, G, HD)
    new_value = my_fresh[:, G * HD :].reshape(row_count, G, HD)
    score_scale = 1.0 / math.sqrt(HD)
    scores = (
        jnp.einsum("ngqd,npgd->ngqp", queries, cached_keys, preferred_element_type=jnp.float32)
        * score_scale
    )
    is_live = (
        jnp.arange(CTX, dtype=jnp.int32)[None, None, None, :] < cached_len[:, None, None, None]
    )
    scores = jnp.where(is_live, scores, -1e30)
    own_score = (
        jnp.einsum("ngqd,ngd->ngq", queries, new_key, preferred_element_type=jnp.float32)
        * score_scale
    )
    row_top = jnp.maximum(jnp.max(scores, axis=-1), own_score)
    weights = jnp.exp(scores - row_top[..., None])
    own_weight = jnp.exp(own_score - row_top)
    denominator = jnp.sum(weights, axis=-1) + own_weight
    weights = (weights / denominator[..., None]).astype(jnp.bfloat16)
    own_weight = (own_weight / denominator).astype(jnp.bfloat16)
    mixture = jnp.einsum(
        "ngqp,npgd->ngqd", weights, cached_values, preferred_element_type=jnp.float32
    )
    mixture = (
        mixture
        + own_weight.astype(jnp.float32)[..., None] * new_value.astype(jnp.float32)[:, :, None, :]
    )
    return mixture.reshape(row_count, H * HD).astype(jnp.bfloat16)


def gates_of(logits, expert_ids):
    labels = jnp.arange(logits.shape[1], dtype=jnp.int32)
    chosen_mask = (expert_ids[:, :, None] == labels[None, None, :]).astype(jnp.float32)
    chosen = jnp.sum(chosen_mask * logits[:, None, :], axis=-1)
    first_gate = 1.0 / (1.0 + jnp.exp(chosen[:, 1] - chosen[:, 0]))
    second_gate = 1.0 / (1.0 + jnp.exp(chosen[:, 0] - chosen[:, 1]))
    return chosen_mask[:, 0, :] * first_gate[:, None] + chosen_mask[:, 1, :] * second_gate[:, None]


def by_width(rows, weight):
    return lax.dot_general(
        rows, weight, (((1,), (1,)), ((), ())), preferred_element_type=jnp.float32
    )


def on_device(
    resid,
    query,
    fresh_kv,
    cache_home,
    kv_cache,
    cached_len,
    wo,
    norm_gain,
    w_router,
    expert_ids,
    w_gate,
    w_up,
    w_down,
):
    slot_count = resid.shape[0]
    tier_count = lax.axis_size("tier")
    head_cols = query.shape[1]
    slot_of = cache_home[0]
    holder = jnp.argsort(slot_of)
    every_query, every_fresh = (
        lax.all_gather(query, "grp", axis=1, tiled=True),
        lax.all_gather(fresh_kv, "grp", axis=1, tiled=True),
    )
    my_rows = lax.dynamic_slice_in_dim(holder, lax.axis_index("grp") * slot_count, slot_count, 0)
    outcome = attend(every_query[my_rows], every_fresh[my_rows], kv_cache, cached_len)
    every_outcome = lax.all_gather(outcome, "grp", axis=0, tiled=True)
    head_rows = lax.dynamic_slice_in_dim(
        every_outcome, lax.axis_index("grp") * head_cols, head_cols, 1
    )
    attended = head_rows[slot_of]
    row_block = attended
    projected = lax.psum_scatter(
        jnp.dot(row_block, wo, preferred_element_type=jnp.float32),
        "grp",
        scatter_dimension=0,
        tiled=True,
    )
    hidden = resid.astype(jnp.float32) + projected
    spread = lax.rsqrt(jnp.mean(hidden * hidden, axis=-1, keepdims=True) + 1e-05)
    normed = (hidden * spread * norm_gain.astype(jnp.float32)[None, :]).astype(jnp.bfloat16)
    gate_weight = w_gate[0]
    up_weight = w_up[0]
    down_weight = w_down[0]
    logits = jnp.dot(normed, w_router, preferred_element_type=jnp.float32)
    gate_table = gates_of(logits, expert_ids)
    tier_rows = lax.all_gather(normed, "tier", axis=0, tiled=True)
    every_rows = lax.all_gather(tier_rows, "grp", axis=0, tiled=True)
    row_block = every_rows
    gate_part = by_width(row_block, gate_weight)
    up_part = by_width(row_block, up_weight)
    activation = (jax.nn.silu(gate_part) * up_part).astype(jnp.bfloat16)
    partial_out = lax.psum_scatter(
        jnp.dot(activation, down_weight, preferred_element_type=jnp.float32),
        "grp",
        scatter_dimension=0,
        tiled=True,
    )
    returned = lax.all_to_all(
        partial_out.astype(jnp.bfloat16), "tier", split_axis=0, concat_axis=0, tiled=True
    ).astype(partial_out.dtype)
    returned = returned.reshape(tier_count, slot_count, returned.shape[1])
    moe = jnp.sum(jnp.transpose(gate_table)[:, :, None] * returned, axis=0)
    return (hidden + moe).astype(jnp.bfloat16)


def solution(mesh):
    return jax.shard_map(
        on_device,
        mesh=mesh,
        in_specs=(
            P(("tier", "grp"), None),
            P("tier", "grp"),
            P("tier", "grp"),
            P("tier", None),
            P(("tier", "grp"), None, None),
            P(("tier", "grp")),
            P("grp", None),
            P(),
            P(),
            P(("tier", "grp"), None),
            P("tier", "grp", None),
            P("tier", "grp", None),
            P("tier", "grp", None),
        ),
        out_specs=P(("tier", "grp"), None),
        check_vma=False,
    )
```

profile of v0, /device:TPU:1, one launch (start us, length us, event | category | flops | bytes accessed | tf_op | source)
XLA Modules:
  0.0 1876.1 jit_solution(12528326055944390275)
XLA Ops:
  6.5 0.0 copy-start
  6.5 0.0 copy-start.5
  6.5 0.0 all-gather.7.cloned.1.call-start
  6.5 0.7 all-gather.7.cloned.1.call-update
  7.3 0.0 all-gather.9.cloned.1.call-start
  7.3 2.8 sort.17
  10.2 0.6 dynamic_slice.6
  12.7 136.0 %all_gather.16 = bf16[64,2048]{0,1:T(8,128)(2,1)S(1)} all-gather(bf16[64,32]{0,1:T(8,128)(2,1)} %param.15), channel_id=1, replica_groups=mesh['tier'=4,'grp'=64] {'grp'}, dimensions={1}, use_global_device_ids=true | all-gather | bytes 266240 | tf_op jit(solution)/shard_map/all_gather | solution.py:88
  148.7 0.8 copy-done.1
  149.5 0.2 dynamic-slice_reduce_fusion
  149.8 1.9 fusion.25
  151.7 1.1 copy.30
  153.4 1.8 copy.31
  155.2 1.2 convert_reduce_fusion
  156.4 51.6 %all-gather.7.cloned.1.call-done = bf16[64,8192]{1,0:T(8,128)(2,1)} async-done(((bf16[64,128]{1,0:T(8,128)(2,1)}), bf16[64,8192]{1,0:T(8,128)(2,1)}) %all-gather.7.cloned.1.call-update) | async-done | bytes 1048592 | tf_op jit(solution)/shard_map/all_gather | solution.py:87
  208.0 1.0 dynamic-slice_reduce_fusion.1
  209.0 0.1 fusion.16
  209.1 0.3 fusion.27
  209.4 0.2 fusion.15
  209.6 1.2 fusion.13
  210.8 0.6 reshape.353
  211.5 0.0 all-gather.9.cloned.1.call-update
  211.5 0.0 all-reduce.5.cloned.1.call-start
  211.5 0.0 copy-done.5
  211.6 287.0 %all-gather.9.cloned.1.call-done = bf16[64,1,8192]{2,1,0:T(2,128)(2,1)} async-done(((bf16[1,1,8192]{2,1,0:T(2,128)(2,1)}), bf16[64,1,8192]{2,1,0:T(2,128)(2,1)}) %all-gather.9.cloned.1.call-update) | async-done | bytes 1048592 | tf_op jit(solution)/shard_map/all_gather | solution.py:92
  498.6 0.8 constant_dynamic-slice_fusion
  499.4 0.6 gather_fusion
  500.0 0.0 copy-start.7
  500.1 0.0 copy-start.2
  500.1 0.0 copy-start.6
  500.1 0.0 copy-start.4
  500.1 3.4 fusion.28
  503.4 0.0 all-reduce.5.cloned.1.call-update
  503.5 0.0 all-gather.11.cloned.1.call-start
  503.5 0.0 copy-done.3
  503.6 0.0 copy-done.7
  503.6 0.6 dynamic-slice.9
  504.2 605.4 %all-reduce.5.cloned.1.call-done = f32[64,8192]{1,0:T(8,128)} async-done(((f32[64,8192]{1,0:T(8,128)}), f32[64,8192]{1,0:T(8,128)}) %all-reduce.5.cloned.1.call-update) | async-done | bytes 2097168
  1109.5 0.0 copy-done.2
  1109.5 2.3 multiply_reduce_fusion.1
  1112.5 52.8 %all-gather.1 = bf16[4,1,8192]{2,1,0:T(2,128)(2,1)S(1)} all-gather(bf16[1,1,8192]{2,1,0:T(2,128)(2,1)S(1)} %convert_bitcast_fusion), channel_id=1, replica_groups=mesh['tier'=4,'grp'=64] {'tier'}, dimensions={0}, use_global_device_ids=true | all-gather | bytes 81920 | tf_op jit(solution)/shard_map/all_gather | solution.py:112
  1165.3 0.7 copy.35
  1166.1 0.0 all-gather.11.cloned.1.call-update
  1166.7 0.0 copy-done.6
  1166.7 0.1 fusion.23
  1166.8 0.0 copy-done.4
  1166.8 0.2 convolution_bitcast_fusion
  1167.0 0.2 select_reduce_fusion
  1167.2 0.6 fusion.26
  1170.4 253.3 %all-gather.11.cloned.1.call-done = bf16[64,4,8192]{2,1,0:T(4,128)(2,1)} async-done(((bf16[1,4,8192]{2,1,0:T(4,128)(2,1)}), bf16[64,4,8192]{2,1,0:T(4,128)(2,1)}) %all-gather.11.cloned.1.call-update) | async-done | bytes 4194320 | tf_op jit(solution)/shard_map/all_gather | solution.py:113
  1423.7 6.9 reshape.358
  1430.6 4.7 fusion.4
  1435.3 0.0 copy-done
  1435.3 11.1 fusion
  1446.5 318.5 %all-reduce.6 = bf16[256,8192]{1,0:T(8,128)(2,1)} all-reduce(f32[256,8192]{1,0:T(8,128)} %fusion), channel_id=3, replica_groups=mesh['tier'=4,'grp'=64] {'grp'}, use_global_device_ids=true, to_apply=%region_6.7.clone | all-reduce | flops 2097152 | bytes 12582912
  1764.9 0.9 fusion.14
  1765.9 0.5 broadcast.179
  1766.4 0.7 reduce.13
  1767.1 0.7 reshape.374
  1767.8 96.0 %all-to-all-start = ((bf16[4,2,4096]{2,1,0:T(2,128)(2,1)}), bf16[4,2,4096]{2,1,0:T(2,128)(2,1)S(1)}, u32[]{:S(2)}, u32[]{:S(2)}) async-start(bf16[4,2,4096]{2,1,0:T(2,128)(2,1)} %reshape.374), calls=%async_computation | async-start | bytes 131072 | tf_op jit(solution)/shard_map/all_to_all | solution.py:124
  1863.8 4.8 all-to-all-done
  1868.6 0.1 reshape.375
  1868.6 0.3 multiply_reduce_fusion
  1868.9 0.7 add_convert_fusion
  (13 shorter events, 0.1 us)
Async XLA Ops:
  6.5 1428.8 %copy-start = (bf16[1,192,8192]{2,1,0:T(8,128)(2,1)S(1)}, bf16[1,192,8192]{2,1,0:T(8,128)(2,1)}, u32[]{:S(2)}) copy-start(bf16[1,192,8192]{2,1,0:T(8,128)(2,1)} %param.25) | copy-start | bytes 9437188
  6.5 205.0 %copy-start.5 = (s32[1,64]{1,0:T(1,128)S(1)}, s32[1,64]{1,0:T(1,128)}, u32[]{:S(2)}) copy-start(s32[1,64]{1,0:T(1,128)} %param.16) | copy-start | bytes 772
  6.5 201.5 %all-gather.7.cloned.1.call-start = ((), (), s32[]{:S(2)}) async-start(), calls=%async_computation.1 | async-start | bytes 1064960 | tf_op jit(solution)/shard_map/all_gather | solution.py:87
  7.3 491.3 %all-gather.9.cloned.1.call-start = ((), (), s32[]{:S(2)}) async-start(), calls=%async_computation.2 | async-start | bytes 2129920 | tf_op jit(solution)/shard_map/all_gather | solution.py:92
  148.7 0.8 copy-start.1
  211.5 898.0 %all-reduce.5.cloned.1.call-start = ((), (), s32[]{:S(2)}) async-start(), calls=%async_computation.4 | async-start | bytes 4194304
  500.0 3.5 copy-start.3
  500.0 3.5 copy-start.7
  500.1 609.5 %copy-start.2 = (bf16[1,8192]{1,0:T(2,128)(2,1)S(1)}, bf16[1,8192]{1,0:T(2,128)(2,1)}, u32[]{:S(2)}) copy-start(bf16[1,8192]{1,0:T(2,128)(2,1)} %param.13) | copy-start | bytes 49156
  500.1 666.7 %copy-start.6 = (s32[1,2]{1,0:T(1,128)S(1)}, s32[1,2]{1,0:T(1,128)}, u32[]{:S(2)}) copy-start(s32[1,2]{1,0:T(1,128)} %param.22) | copy-start | bytes 28
  500.1 666.7 %copy-start.4 = (bf16[8192,4]{0,1:T(4,128)(2,1)S(1)}, bf16[8192,4]{0,1:T(4,128)(2,1)}, u32[]{:S(2)}) copy-start(bf16[8192,4]{0,1:T(4,128)(2,1)} %param.21) | copy-start | bytes 196612
  503.5 920.2 %all-gather.11.cloned.1.call-start = ((), (), s32[]{:S(2)}) async-start(), calls=%async_computation.3 | async-start | bytes 4259840 | tf_op jit(solution)/shard_map/all_gather | solution.py:113
  1767.8 100.8 %all-to-all-start = ((bf16[4,2,4096]{2,1,0:T(2,128)(2,1)}), bf16[4,2,4096]{2,1,0:T(2,128)(2,1)S(1)}, u32[]{:S(2)}, u32[]{:S(2)}) async-start(bf16[4,2,4096]{2,1,0:T(2,128)(2,1)} %reshape.374), calls=%async_computation | async-start | bytes 131072 | tf_op jit(solution)/shard_map/all_to_all | solution.py:124
Sparse Core Ops, SparseCore 0:
  9.1 198.8 all-gather.6
  211.6 286.9 all-gather.8
  503.6 605.9 all-reduce.4
  1166.2 257.4 all-gather.10
where the time goes:
time: 1880 us
  waiting for transfers between devices  1200 us (64%)
  blocking collectives  507 us (27%)
  starting transfers between devices  96.1 us (5%)
  matrix products  21 us (1%)
  local copies, waits for them, and re-layouts  20.6 us (1%)
  between operations  19.8 us (1%)
    unnamed x5, waiting for transfers between devices  606 us
    unnamed x1, blocking collectives  318 us
    all_gather x1, waiting for transfers between devices, on_device(): every_outcome = lax.all_gather(outcome, 'grp', axis=0, tiled=True)  287 us
    all_gather x1, waiting for transfers between devices, on_device(): every_rows = lax.all_gather(tier_rows, 'grp', axis=0, tiled=True)  253 us
    all_gather x1, blocking collectives, on_device(): lax.all_gather(fresh_kv, 'grp', axis=1, tiled=True)  136 us
    all_to_all x1, starting transfers between devices, on_device(): lax.all_to_all(partial_out.astype(jnp.bfloat16), 'tier', split_axis=0, co...  96 us
    all_gather x1, blocking collectives, on_device(): tier_rows = lax.all_gather(normed, 'tier', axis=0, tiled=True)  52.8 us
    all_gather x1, waiting for transfers between devices, on_device(): lax.all_gather(query, 'grp', axis=1, tiled=True)  51.6 us
  transfers between devices with their start and end apart: 5, of which 5 were waited for; matrix products, arithmetic and copies ran while one was open for 1% of the time, Pallas kernels for 0%

commit v1 on v0

v1 whole, which is shorter than its diff:
```python
import functools
import math

import jax
import jax.numpy as jnp
from jax import lax
from jax.experimental import pallas as pl
from jax.experimental.pallas import tpu as pltpu
from jax.sharding import PartitionSpec as P

MESH = pl.DeviceIdType.MESH
F32 = jnp.float32
BF16 = jnp.bfloat16
CZ = 3072
CX = 8192 - CZ
SZ = CZ // 128
SX = CX // 128
TN = 512


def iota(shape, dim):
    return lax.broadcasted_iota(jnp.int32, shape, dim)


def nt(a, b):
    return lax.dot_general(a, b, (((1,), (1,)), ((), ())), preferred_element_type=F32)


def nn(a, b):
    return jnp.dot(a, b, preferred_element_type=F32)


def kernel(
    home_ref, len_ref, ids_ref, query_ref, fresh_ref, resid_ref, gain_ref, router_ref,
    cache_hbm, wo_hbm, gate_hbm, up_hbm, down_hbm,
    out_ref,
    cache, wo, w_in, w_down, local_sem,
    a1s, a1r, a2s, a2r, c1s, c1r, c2s, c2r,
    r1zs, r1zr, r1xs, r1xr, r2zs, r2zr, r2xs, r2xr,
    hid, g1s, g1r, g1f, xa, xb, acc, act,
    f0s, f0r, f1s, f1ra, f1rb, f2sa, f2sb, f2ra, f2rb, f3f, f3s, f3r,
    sa1, sa2, sc1, sc2, sr1z, sr1x, sr2z, sr2x, sg1, sg2, sg3, sg4, sf0, sf1, sf2, sf3,
):
    tier, grp = lax.axis_index("tier"), lax.axis_index("grp")
    y_hi, core = tier // 2, tier % 2
    y_lo, z, x = grp // 32, (grp // 4) % 8, grp % 4
    y = y_hi * 2 + y_lo
    xy = y_lo * 4 + x
    zc = z * 2 + core

    def device(y, z, x, core):
        return ((y // 2) * 2 + core, (y % 2) * 32 + z * 4 + x)

    def send(src, dst, sems, k, to):
        copy = pltpu.make_async_remote_copy(
            src_ref=src, dst_ref=dst, send_sem=sems.at[0, k], recv_sem=sems.at[1, k],
            device_id=to, device_id_type=MESH,
        )
        copy.start()
        return copy

    z_peers = [((z + k) % 8, device(y, (z + k) % 8, x, core)) for k in range(1, 8)]
    xy_peers = []
    for k in range(1, 8):
        px, pl_lo = (x + k) % 4, (y_lo + k // 4) % 2
        xy_peers.append((pl_lo * 4 + px, device(y_hi * 2 + pl_lo, z, px, core)))
    zc_peers = []
    for k in range(1, 16):
        pz, pc = (z + k // 2) % 8, (core + k % 2) % 2
        zc_peers.append((pz * 2 + pc, device(y, pz, x, pc)))
    x_peers = [((x + k) % 4, device(y, z, (x + k) % 4, core)) for k in range(1, 4)]
    y_peers = [((y + k) % 4, device((y + k) % 4, z, x, core)) for k in range(1, 4)]
    sibling = device(y, z, x, 1 - core)
    far = [device(((1 - y_hi) * 2 + (y_lo + k) % 2), z, x, core) for k in range(2)]

    loads = [
        pltpu.make_async_copy(cache_hbm.at[0], cache, local_sem.at[0]),
        pltpu.make_async_copy(wo_hbm, wo, local_sem.at[1]),
        pltpu.make_async_copy(gate_hbm.at[0], w_in.at[0], local_sem.at[2]),
        pltpu.make_async_copy(up_hbm.at[0], w_in.at[1], local_sem.at[3]),
        pltpu.make_async_copy(down_hbm.at[0], w_down, local_sem.at[4]),
    ]
    for load in loads:
        load.start()

    barrier = pltpu.get_barrier_semaphore()
    greeted = [d for _, d in zc_peers] + [d for _, d in xy_peers] + far
    for d in greeted:
        pl.semaphore_signal(barrier, inc=1, device_id=d, device_id_type=MESH)

    slot = home_ref[...]
    place = ((slot >> 2) & 7) * 8 + (slot >> 5) * 4 + (slot & 3)
    to_slot = (iota((64, 64), 0) == place).astype(BF16)
    spread_fresh = (iota((32, 128), 1) == iota((32, 128), 0) + 32 * x).astype(BF16)
    fresh_wide = nn(fresh_ref[...], spread_fresh).astype(BF16)
    by_slot_q = nn(to_slot, query_ref[...])
    by_slot_f = nn(to_slot, fresh_wide)
    for k in range(8):
        a1s[k * 16 : k * 16 + 8] = by_slot_q[k * 8 : k * 8 + 8]
        a1s[k * 16 + 8 : k * 16 + 16] = by_slot_f[k * 8 : k * 8 + 8]

    pl.semaphore_wait(barrier, len(greeted))

    def rows(ref, i, n):
        return ref.at[pl.ds(pl.multiple_of(i * n, n), n)]

    pending = []
    copies = [
        send(rows(a1s, p, 16), rows(a1r, z, 16), sa1, k, d) for k, (p, d) in enumerate(z_peers)
    ]
    rows(a1r, z, 16)[...] = rows(a1s, z, 16)[...]
    for c in copies:
        c.wait_recv()
    pending += copies
    for k in range(8):
        for half in range(2):
            a2s[k * 16 + half * 8 : k * 16 + half * 8 + 8] = a1r[pl.ds(half * 8 + k, 8, stride=16), :]
    copies = [
        send(rows(a2s, p, 16), rows(a2r, xy, 16), sa2, k, d) for k, (p, d) in enumerate(xy_peers)
    ]
    rows(a2r, xy, 16)[...] = rows(a2s, xy, 16)[...]
    for c in copies:
        c.wait_recv()
    pending += copies

    head = iota((64, 128), 0)
    group = (head >> 5) * 4 + ((head & 7) >> 1)
    got = a2r[...].reshape(8, 16, 128)
    queries = got[:, :8].reshape(64, 128)
    news = got[:, 8:]
    new_key = (news[0] + news[1] + news[2] + news[3]).astype(BF16)
    new_value = (news[4] + news[5] + news[6] + news[7]).astype(BF16)
    of_group = (iota((64, 8), 1) == (iota((64, 8), 0) >> 5) * 4 + ((iota((64, 8), 0) & 7) >> 1)).astype(BF16)
    own_key = nn(of_group, new_key)
    own_value = nn(of_group, new_value)
    loads[0].wait()
    wide = jnp.concatenate(
        [jnp.where(group == j, queries, 0.0).astype(BF16) for j in range(8)], axis=1
    )
    scale = 1.0 / math.sqrt(128)
    scores = nt(wide, cache[:, :1024]) * scale
    scores = jnp.where(iota((64, 128), 1) < len_ref[0], scores, -1e30)
    own_score = jnp.sum(queries * own_key, axis=1, keepdims=True) * scale
    top = jnp.maximum(jnp.max(scores, axis=1, keepdims=True), own_score)
    weights = jnp.exp(scores - top)
    own_weight = jnp.exp(own_score - top)
    denominator = jnp.sum(weights, axis=1, keepdims=True) + own_weight
    weights = (weights / denominator).astype(BF16)
    own_weight = (own_weight / denominator).astype(BF16).astype(F32)
    mixed = nn(weights, cache[:, 1024:])
    outcome = own_weight * own_value
    for j in range(8):
        outcome = outcome + jnp.where(group == j, mixed[:, j * 128 : (j + 1) * 128], 0.0)
    c1s[...] = outcome.astype(BF16).astype(F32)

    copies = [
        send(rows(c1s, p, 8), rows(c1r, xy, 8), sc1, k, d) for k, (p, d) in enumerate(xy_peers)
    ]
    rows(c1r, xy, 8)[...] = rows(c1s, xy, 8)[...]
    for c in copies:
        c.wait_recv()
    pending += copies
    for k in range(8):
        c2s[k * 8 : k * 8 + 8] = c1r[pl.ds(k, 8, stride=8), :]
    copies = [
        send(rows(c2s, p, 8), rows(c2r, z, 8), sc2, k, d) for k, (p, d) in enumerate(z_peers)
    ]
    rows(c2r, z, 8)[...] = rows(c2s, z, 8)[...]
    for c in copies:
        c.wait_recv()
    pending += copies

    own = iota((64, 64), 1)
    own_z, own_xy = (own >> 2) & 7, (own >> 5) * 4 + (own & 3)
    by_head = c2r[...].astype(BF16)
    order_z = (iota((64, 64), 0) == own_z * 8 + own_xy).astype(BF16)
    order_x = (iota((64, 64), 0) == own_xy * 8 + own_z).astype(BF16)
    att_z = nn(nt(order_z, to_slot).astype(BF16), by_head).astype(BF16)
    att_x = nn(nt(order_x, to_slot).astype(BF16), by_head).astype(BF16)
    loads[1].wait()

    def project(att, ref, base, width):
        def tile(t, _):
            at = pl.multiple_of(t * TN, TN)
            lo = nn(att, wo[:, pl.ds(base + at, TN)]).reshape(8, 8, TN)
            hi = nn(att, wo[:, pl.ds(base + width + at, TN)]).reshape(8, 8, TN)
            ref[:, :, pl.ds(at, TN)] = jnp.concatenate([lo, hi], axis=1).astype(BF16)
            return 0

        lax.fori_loop(0, width // TN, tile, 0)

    project(att_z, r1zs, 0, CZ // 2)
    copies_z = [send(r1zs.at[p], r1zr.at[k], sr1z, k, d) for k, (p, d) in enumerate(z_peers)]
    project(att_x, r1xs, CZ, CX // 2)
    copies_x = [send(r1xs.at[p], r1xr.at[k], sr1x, k, d) for k, (p, d) in enumerate(xy_peers)]
    pending += copies_z + copies_x

    def fold(sent, mine, received, n, slabs, stride):
        def tile(j, _):
            at = pl.multiple_of(j * 128, 128)
            total = sent[mine, :, pl.ds(at, 128)].astype(F32)
            for k in range(n):
                total = total + received[k, :, pl.ds(at, 128)].astype(F32)
            slabs[pl.ds(j, 8, stride=stride), :] = total[:8]
            slabs[pl.ds(j + stride // 2, 8, stride=stride), :] = total[8:]
            return 0

        lax.fori_loop(0, stride // 2, tile, 0)

    for c in copies_z:
        c.wait_recv()
    fold(r1zs, z, r1zr, 7, r2zs, SZ)
    copies_z = [
        send(rows(r2zs, p, SZ), r2zr.at[k], sr2z, k, d) for k, (p, d) in enumerate(xy_peers)
    ]
    for c in copies_x:
        c.wait_recv()
    fold(r1xs, xy, r1xr, 7, r2xs, SX)
    copies_x = [
        send(rows(r2xs, p, SX), r2xr.at[k], sr2x, k, d) for k, (p, d) in enumerate(z_peers)
    ]
    for c in copies_z + copies_x:
        c.wait_recv()
    pending += copies_z + copies_x
    part_z, part_x = rows(r2zs, xy, SZ)[...], rows(r2xs, z, SX)[...]
    for k in range(7):
        part_z = part_z + r2zr[k]
        part_x = part_x + r2xr[k]
    hidden = resid_ref[...].astype(F32) + jnp.concatenate([part_z, part_x], axis=0)
    hid[...] = hidden

    mean = jnp.sum(hidden * hidden, keepdims=True) * (1.0 / 8192)
    normed = (hidden * lax.rsqrt(mean + 1e-05) * gain_ref[...].astype(F32)).astype(BF16)
    normed_wide = normed.astype(F32)
    logits = [
        jnp.sum(normed_wide * router_ref[e].astype(F32), keepdims=True) for e in range(4)
    ]
    first, second = ids_ref[0, 0], ids_ref[0, 1]
    zero = jnp.zeros((1, 1), F32)
    logit_a, logit_b = zero, zero
    for e in range(4):
        logit_a = logit_a + jnp.where(first == e, logits[e], zero)
        logit_b = logit_b + jnp.where(second == e, logits[e], zero)
    gate_a = 1.0 / (1.0 + jnp.exp(logit_b - logit_a))
    gate_b = 1.0 / (1.0 + jnp.exp(logit_a - logit_b))
    lane = iota((16, 128), 1)
    gate_row = jnp.where((lane & 3) == first, gate_a, 0.0) + jnp.where((lane & 3) == second, gate_b, 0.0)
    gate_high = gate_row.astype(BF16).astype(F32)
    gate_pair = jnp.where(lane < 4, gate_high, jnp.where(lane < 8, gate_row - gate_high, 0.0)).astype(BF16)
    for c in range(2):
        g1s[c * 48 : c * 48 + 32] = normed[c * 32 : c * 32 + 32]
        g1s[c * 48 + 32 : c * 48 + 48] = gate_pair

    copies = []
    for k, (p, d) in enumerate(zc_peers):
        copies.append(send(rows(g1s, p % 2, 48), rows(g1r, zc, 48), sg1, k, d))
    rows(g1r, zc, 48)[...] = rows(g1s, core, 48)[...]
    for c in copies:
        c.wait_recv()
    pending += copies
    g1f[...] = g1r[...].astype(F32)
    for j in range(16):
        xa[core, y, x, :, j * 128 : j * 128 + 128] = g1f[pl.ds(j, 16, stride=48), :].astype(BF16)
    for j in range(17):
        xb[core, y, x, :, j * 128 : j * 128 + 128] = g1f[pl.ds(16 + j, 16, stride=48), :].astype(BF16)

    first_a = [send(xa.at[core, y, x], xa.at[core, y, x], sg2, k, d) for k, (p, d) in enumerate(y_peers)]
    first_b = [send(xb.at[core, y, x], xb.at[core, y, x], sg2, 3 + k, d) for k, (p, d) in enumerate(x_peers)]
    for c in first_a + first_b:
        c.wait_recv()
    then_a = [send(xa.at[core, :, x], xa.at[core, :, x], sg3, k, d) for k, (p, d) in enumerate(x_peers)]
    then_b = [send(xb.at[core, y], xb.at[core, y], sg3, 3 + k, d) for k, (p, d) in enumerate(y_peers)]
    across = [
        send(xa.at[core, :, x], xa.at[core, :, x], sg4, 0, sibling),
        send(xb.at[core, y], xb.at[core, y], sg4, 4, sibling),
    ]
    for k in range(3):
        from_x, from_y = (x + 3 - k) % 4, (y + 3 - k) % 4
        then_a[k].wait_recv()
        across.append(send(xa.at[core, :, from_x], xa.at[core, :, from_x], sg4, 1 + k, sibling))
        then_b[k].wait_recv()
        across.append(send(xb.at[core, from_y], xb.at[core, from_y], sg4, 5 + k, sibling))
    pending += first_a + first_b + then_a + then_b + across

    for load in loads[2:]:
        load.wait()
    acc[...] = jnp.zeros_like(acc)

    def into(half):
        def tile(t, _):
            at = pl.multiple_of(t * TN, TN)
            for part, ref in ((0, xa), (1, xb)):
                rows_in = ref[half, :, :, :, pl.ds(at, TN)].reshape(256, TN)
                column = pl.ds(pl.multiple_of(half * 4096 + part * 2048 + at, TN), TN)
                acc[0] += nt(rows_in, w_in[0, :, column])
                acc[1] += nt(rows_in, w_in[1, :, column])
            return 0

        lax.fori_loop(0, 2048 // TN, tile, 0)

    into(core)
    for c in across:
        c.wait_recv()
    into(1 - core)
    gate_part = acc[0]
    act[...] = (gate_part / (1.0 + jnp.exp(-gate_part)) * acc[1]).astype(BF16)
    pairs = xb[core, :, :, :, 2048:].reshape(256, 128).astype(F32)
    mine = (iota((256, 128), 1) & 3) == tier
    gate = jnp.sum(jnp.where(mine, pairs, 0.0), axis=1, keepdims=True)

    def down(column):
        return nn(act[...], w_down[:, column]) * gate

    over = []
    for part in range(2):
        def tile(t, _, part=part):
            at = pl.multiple_of(t * TN, TN)
            column = pl.ds(pl.multiple_of((1 - core) * 4096 + part * 2048 + at, TN), TN)
            f0s[part, :, :, :, pl.ds(at, TN)] = down(column).astype(BF16).reshape(4, 4, 16, TN)
            return 0

        lax.fori_loop(0, 2048 // TN, tile, 0)
        over.append(send(f0s.at[part], f0r.at[part], sf0, part, sibling))
    pending += over

    then = []
    for part in range(2):
        over[part].wait_recv()

        def tile(t, _, part=part):
            at = pl.multiple_of(t * TN, TN)
            column = pl.ds(pl.multiple_of(core * 4096 + part * 2048 + at, TN), TN)
            both = down(column) + f0r[part, :, :, :, pl.ds(at, TN)].reshape(256, TN).astype(F32)
            f1s[part, :, :, :, pl.ds(at, TN)] = both.astype(BF16).reshape(4, 4, 16, TN)
            return 0

        lax.fori_loop(0, 2048 // TN, tile, 0)
        if part == 0:
            then.append([send(f1s.at[0, :, p], f1ra.at[k], sf1, k, d) for k, (p, d) in enumerate(x_peers)])
        else:
            then.append([send(f1s.at[1, p], f1rb.at[k], sf1, 3 + k, d) for k, (p, d) in enumerate(y_peers)])
    pending += then[0] + then[1]

    last = []
    for part in range(2):
        for c in then[part]:
            c.wait_recv()

        def tile(t, _, part=part):
            at = pl.ds(pl.multiple_of(t * TN, TN), TN)
            if part == 0:
                total = f1s[0, :, x, :, at].astype(F32)
                for k in range(3):
                    total = total + f1ra[k, :, :, at].astype(F32)
                f2sa[:, :, at] = total.astype(BF16)
            else:
                total = f1s[1, y, :, :, at].astype(F32)
                for k in range(3):
                    total = total + f1rb[k, :, :, at].astype(F32)
                f2sb[:, :, at] = total.astype(BF16)
            return 0

        lax.fori_loop(0, 2048 // TN, tile, 0)
        if part == 0:
            last.append([send(f2sa.at[p], f2ra.at[k], sf2, k, d) for k, (p, d) in enumerate(y_peers)])
        else:
            last.append([send(f2sb.at[p], f2rb.at[k], sf2, 3 + k, d) for k, (p, d) in enumerate(x_peers)])
    pending += last[0] + last[1]
    for c in last[0] + last[1]:
        c.wait_recv()
    for j in range(16):
        at = slice(j * 128, j * 128 + 128)
        total_a, total_b = f2sa[y, :, at].astype(F32), f2sb[x, :, at].astype(F32)
        for k in range(3):
            total_a = total_a + f2ra[k, :, at].astype(F32)
            total_b = total_b + f2rb[k, :, at].astype(F32)
        f3f[pl.ds(j, 16, stride=32), :] = total_a
        f3f[pl.ds(16 + j, 16, stride=32), :] = total_b
    f3s[...] = f3f[...].astype(BF16)
    copies = [send(rows(f3s, p, 32), f3r.at[zc], sf3, k, d) for k, (p, d) in enumerate(zc_peers)]
    f3r[zc] = rows(f3s, zc, 32)[...]
    for c in copies:
        c.wait_recv()
    pending += copies
    low, high = f3r[0].astype(F32), f3r[1].astype(F32)
    for k in range(1, 8):
        low = low + f3r[2 * k].astype(F32)
        high = high + f3r[2 * k + 1].astype(F32)
    out_ref[...] = (hid[...] + jnp.concatenate([low, high], axis=0)).astype(BF16)
    for c in pending:
        c.wait_send()


def on_device(
    resid, query, fresh_kv, cache_home, kv_cache, cached_len, wo, norm_gain, w_router,
    expert_ids, w_gate, w_up, w_down,
):
    vmem, smem, hbm = (
        pl.BlockSpec(memory_space=pltpu.VMEM),
        pl.BlockSpec(memory_space=pltpu.SMEM),
        pl.BlockSpec(memory_space=pl.ANY),
    )
    v = pltpu.VMEM
    sem = lambda n: pltpu.SemaphoreType.DMA((2, n))
    out = pl.pallas_call(
        kernel,
        out_shape=jax.ShapeDtypeStruct((64, 128), BF16),
        in_specs=[vmem, smem, smem, vmem, vmem, vmem, vmem, vmem, hbm, hbm, hbm, hbm, hbm],
        out_specs=vmem,
        scratch_shapes=[
            v((128, 2048), BF16), v((128, 8192), BF16), v((2, 192, 8192), BF16), v((192, 8192), BF16),
            pltpu.SemaphoreType.DMA((5,)),
            v((128, 128), F32), v((128, 128), F32), v((128, 128), F32), v((128, 128), F32),
            v((64, 128), F32), v((64, 128), F32), v((64, 128), F32), v((64, 128), F32),
            v((8, 16, CZ // 2), BF16), v((7, 16, CZ // 2), BF16),
            v((8, 16, CX // 2), BF16), v((7, 16, CX // 2), BF16),
            v((8 * SZ, 128), F32), v((7, SZ, 128), F32), v((8 * SX, 128), F32), v((7, SX, 128), F32),
            v((64, 128), F32), v((96, 128), BF16), v((768, 128), BF16), v((768, 128), F32),
            v((2, 4, 4, 16, 2048), BF16), v((2, 4, 4, 16, 2176), BF16),
            v((2, 256, 192), F32), v((256, 192), BF16),
            v((2, 4, 4, 16, 2048), BF16), v((2, 4, 4, 16, 2048), BF16), v((2, 4, 4, 16, 2048), BF16),
            v((3, 4, 16, 2048), BF16), v((3, 4, 16, 2048), BF16),
            v((4, 16, 2048), BF16), v((4, 16, 2048), BF16), v((3, 16, 2048), BF16), v((3, 16, 2048), BF16),
            v((512, 128), F32), v((512, 128), BF16), v((16, 32, 128), BF16),
            sem(7), sem(7), sem(7), sem(7), sem(7), sem(7), sem(7), sem(7),
            sem(15), sem(6), sem(6), sem(8), sem(2), sem(6), sem(6), sem(15),
        ],
        compiler_params=pltpu.CompilerParams(
            collective_id=0, has_side_effects=True, vmem_limit_bytes=60 * 2**20
        ),
    )(
        cache_home, cached_len, expert_ids, query, fresh_kv, resid.reshape(64, 128),
        norm_gain.reshape(64, 128), jnp.transpose(w_router).reshape(4, 64, 128),
        kv_cache, wo, w_gate, w_up, w_down,
    )
    return out.reshape(1, 8192)


def solution(mesh):
    return jax.shard_map(
        on_device,
        mesh=mesh,
        in_specs=(
            P(("tier", "grp"), None),
            P("tier", "grp"),
            P("tier", "grp"),
            P("tier", None),
            P(("tier", "grp"), None, None),
            P(("tier", "grp")),
            P("grp", None),
            P(),
            P(),
            P(("tier", "grp"), None),
            P("tier", "grp", None),
            P("tier", "grp", None),
            P("tier", "grp", None),
        ),
        out_specs=P(("tier", "grp"), None),
        check_vma=False,
    )
```

time: 1880 us -> 120 us (0.06)
  waiting for transfers between devices: 1200 us -> 0 us
  blocking collectives: 507 us -> 0 us
  Pallas kernels: 0 us -> 113 us
  starting transfers between devices: 96.1 us -> 0 us
  matrix products: 21 us -> 0 us
  between operations: 19.8 us -> 0.66 us
    unnamed x5 -> x0, waiting for transfers between devices: 606 us -> none
    all_gather x3 -> x0, waiting for transfers between devices: 592 us -> none  [the longest x1 287 us: on_device(): every_outcome = lax.all_gather(outcome, 'grp', axis=0, tiled=True)]
    unnamed x1 -> x0, blocking collectives: 318 us -> none
    all_gather x2 -> x0, blocking collectives: 189 us -> none  [the longest x1 136 us: on_device(): lax.all_gather(fresh_kv, 'grp', axis=1, tiled=True)]
    pallas_call x0 -> x1, Pallas kernels: none -> 113 us  [on_device(): pl.pallas_call(kernel, out_shape=jax.ShapeDtypeStruct((64, 128), BF16), i...]
    all_to_all x1 -> x0, starting transfers between devices: 96 us -> none  [on_device(): lax.all_to_all(partial_out.astype(jnp.bfloat16), 'tier', split_axis=0, co...]
    dot_general x7 -> x0, matrix products: 21 us -> none  [the longest x1 11.1 us: on_device(): jnp.dot(activation, down_weight, preferred_element_type=jnp.float32)]
  transfers between devices with their start and end apart: 5 -> 0, of which waited for: 5 -> 0; matrix products, arithmetic and copies ran while one was open for 1% -> 0% of each run, Pallas kernels for 0% -> 0%
where the time goes in v1:
time: 120 us
  Pallas kernels  113 us (94%)
  local copies, waits for them, and re-layouts  4.21 us (4%)
  other arithmetic  1.45 us (1%)
    pallas_call x1, Pallas kernels, on_device(): pl.pallas_call(kernel, out_shape=jax.ShapeDtypeStruct((64, 128), BF16), i...  113 us
    unnamed x3, local copies, waits for them, and re-layouts  4.21 us

profile of v1, /device:TPU:1, one launch (start us, length us, event | category | flops | bytes accessed | tf_op | source)
XLA Modules:
  0.0 119.7 jit_solution(8745353480103968420)
XLA Ops:
  0.7 1.4 %reduce = bf16[8192]{0:T(1024)(128)(2,1)} reduce(bf16[1,8192]{1,0:T(2,128)(2,1)} %param.13, bf16[]{:T(256)} %constant.9), dimensions={0}, to_apply=%param.13.reduce_sub_computation | reduce | bytes 32770 | tf_op args[0]
  2.1 1.4 %copy.14.fresh_ref = bf16[64,32]{1,0:T(8,128)(2,1)} copy(bf16[64,32]{0,1:T(8,128)(2,1)} %param.15) | data formatting | bytes 8192 | tf_op args[2]
  3.5 1.5 %copy.19 = bf16[1,4,64,128]{3,2,1,0:T(8,128)(2,1)} copy(bf16[1,4,64,128]{3,1,2,0:T(4,128)(2,1)} %bitcast.15) | data formatting | bytes 131072
  5.0 113.4 %shard_map.127 = bf16[64,128]{1,0:T(8,128)(2,1)} custom-call(s32[1,64]{1,0:T(1,128)} %home_ref.1, s32[1]{0:T(128)S(6)} %copy.21.len_ref, s32[1,2]{1,0:T(1,128)} %ids_ref.1, bf16[64,128]{1,0:T(8,128)(2,1)} %query_ref.1, bf16[64,32]{1,0:T(8,128)(2,1)} %copy.14.fresh_ref, bf16[64,128]{1,0:T(8,128)(2,1)} %bitcast.13, bf16[64,128]{1,0:T(8,128)(2,1)} %bitcast.16, ...), custom_call_target="tpu_custom_call" | custom-call | tf_op jit(solution)/shard_map/pallas_call | solution.py:405
  118.3 1.4 %copy.20 = bf16[1,1,64,128]{3,1,2,0:T(2,128)(2,1)} copy(bf16[1,1,64,128]{3,2,1,0:T(8,128)(2,1)} %bitcast.14) | data formatting | bytes 32768

commit v2 on v1

--- a/solution.py
+++ b/solution.py
@@ -15,6 +15,7 @@
 CX = 8192 - CZ
 SZ = CZ // 128
 SX = CX // 128
+PZ, PX = -(-SZ // 16) * 16, -(-SX // 16) * 16
 TN = 512
 
 
@@ -37,9 +38,10 @@
     cache, wo, w_in, w_down, local_sem,
     a1s, a1r, a2s, a2r, c1s, c1r, c2s, c2r,
     r1zs, r1zr, r1xs, r1xr, r2zs, r2zr, r2xs, r2xr,
-    hid, g1s, g1r, g1f, xa, xb, acc, act,
-    f0s, f0r, f1s, f1ra, f1rb, f2sa, f2sb, f2ra, f2rb, f3f, f3s, f3r,
-    sa1, sa2, sc1, sc2, sr1z, sr1x, sr2z, sr2x, sg1, sg2, sg3, sg4, sf0, sf1, sf2, sf3,
+    r2fz, r2fx, hid, router,
+    g1s, g1r, g1f, gates, gate_in, gate_all, xa, xb, acc, act,
+    f0s, f0r, f1s, fo, fd, fcs, fcr, f2s, f2r, f3f, f3s, f3r,
+    sa1, sa2, sc1, sc2, sr1z, sr1x, sr2z, sr2x, sg1, sgate, sg2, sg3, sg4, sf0, sf1, sf2, sf3,
 ):
     tier, grp = lax.axis_index("tier"), lax.axis_index("grp")
     y_hi, core = tier // 2, tier % 2
@@ -92,12 +94,18 @@
     place = ((slot >> 2) & 7) * 8 + (slot >> 5) * 4 + (slot & 3)
     to_slot = (iota((64, 64), 0) == place).astype(BF16)
     spread_fresh = (iota((32, 128), 1) == iota((32, 128), 0) + 32 * x).astype(BF16)
-    fresh_wide = nn(fresh_ref[...], spread_fresh).astype(BF16)
     by_slot_q = nn(to_slot, query_ref[...])
-    by_slot_f = nn(to_slot, fresh_wide)
+    by_slot_f = nn(nt(to_slot, fresh_ref[...]).astype(BF16), spread_fresh)
     for k in range(8):
         a1s[k * 16 : k * 16 + 8] = by_slot_q[k * 8 : k * 8 + 8]
         a1s[k * 16 + 8 : k * 16 + 16] = by_slot_f[k * 8 : k * 8 + 8]
+
+    resid_row, router_rows = resid_ref[...].astype(F32), router_ref[...].astype(F32)
+    for j in range(64):
+        hid[j : j + 1] = resid_row[:, j * 128 : j * 128 + 128]
+        router[pl.ds(j, 4, stride=64), :] = router_rows[:, j * 128 : j * 128 + 128]
+    r2fz[...] = jnp.zeros_like(r2fz)
+    r2fx[...] = jnp.zeros_like(r2fx)
 
     pl.semaphore_wait(barrier, len(greeted))
 
@@ -195,45 +203,47 @@
     copies_x = [send(r1xs.at[p], r1xr.at[k], sr1x, k, d) for k, (p, d) in enumerate(xy_peers)]
     pending += copies_z + copies_x
 
-    def fold(sent, mine, received, n, slabs, stride):
+    def fold(sent, mine, received, n, slabs, used, stride):
         def tile(j, _):
             at = pl.multiple_of(j * 128, 128)
             total = sent[mine, :, pl.ds(at, 128)].astype(F32)
             for k in range(n):
                 total = total + received[k, :, pl.ds(at, 128)].astype(F32)
             slabs[pl.ds(j, 8, stride=stride), :] = total[:8]
-            slabs[pl.ds(j + stride // 2, 8, stride=stride), :] = total[8:]
+            slabs[pl.ds(j + used // 2, 8, stride=stride), :] = total[8:]
             return 0
 
-        lax.fori_loop(0, stride // 2, tile, 0)
+        lax.fori_loop(0, used // 2, tile, 0)
 
     for c in copies_z:
         c.wait_recv()
-    fold(r1zs, z, r1zr, 7, r2zs, SZ)
+    fold(r1zs, z, r1zr, 7, r2fz, SZ, PZ)
+    r2zs[...] = r2fz[...].astype(BF16)
     copies_z = [
-        send(rows(r2zs, p, SZ), r2zr.at[k], sr2z, k, d) for k, (p, d) in enumerate(xy_peers)
+        send(rows(r2zs, p, PZ), r2zr.at[k], sr2z, k, d) for k, (p, d) in enumerate(xy_peers)
     ]
     for c in copies_x:
         c.wait_recv()
-    fold(r1xs, xy, r1xr, 7, r2xs, SX)
+    fold(r1xs, xy, r1xr, 7, r2fx, SX, PX)
+    r2xs[...] = r2fx[...].astype(BF16)
     copies_x = [
-        send(rows(r2xs, p, SX), r2xr.at[k], sr2x, k, d) for k, (p, d) in enumerate(z_peers)
+        send(rows(r2xs, p, PX), r2xr.at[k], sr2x, k, d) for k, (p, d) in enumerate(z_peers)
     ]
     for c in copies_z + copies_x:
         c.wait_recv()
     pending += copies_z + copies_x
-    part_z, part_x = rows(r2zs, xy, SZ)[...], rows(r2xs, z, SX)[...]
+    part_z, part_x = rows(r2fz, xy, PZ)[...], rows(r2fx, z, PX)[...]
     for k in range(7):
-        part_z = part_z + r2zr[k]
-        part_x = part_x + r2xr[k]
-    hidden = resid_ref[...].astype(F32) + jnp.concatenate([part_z, part_x], axis=0)
+        part_z = part_z + r2zr[k].astype(F32)
+        part_x = part_x + r2xr[k].astype(F32)
+    hidden = hid[...] + jnp.concatenate([part_z[:SZ], part_x[:SX]], axis=0)
     hid[...] = hidden
 
     mean = jnp.sum(hidden * hidden, keepdims=True) * (1.0 / 8192)
     normed = (hidden * lax.rsqrt(mean + 1e-05) * gain_ref[...].astype(F32)).astype(BF16)
     normed_wide = normed.astype(F32)
     logits = [
-        jnp.sum(normed_wide * router_ref[e].astype(F32), keepdims=True) for e in range(4)
+        jnp.sum(normed_wide * router[e * 64 : e * 64 + 64], keepdims=True) for e in range(4)
     ]
     first, second = ids_ref[0, 0], ids_ref[0, 1]
     zero = jnp.zeros((1, 1), F32)
@@ -243,44 +253,101 @@
         logit_b = logit_b + jnp.where(second == e, logits[e], zero)
     gate_a = 1.0 / (1.0 + jnp.exp(logit_b - logit_a))
     gate_b = 1.0 / (1.0 + jnp.exp(logit_a - logit_b))
-    lane = iota((16, 128), 1)
-    gate_row = jnp.where((lane & 3) == first, gate_a, 0.0) + jnp.where((lane & 3) == second, gate_b, 0.0)
-    gate_high = gate_row.astype(BF16).astype(F32)
-    gate_pair = jnp.where(lane < 4, gate_high, jnp.where(lane < 8, gate_row - gate_high, 0.0)).astype(BF16)
-    for c in range(2):
-        g1s[c * 48 : c * 48 + 32] = normed[c * 32 : c * 32 + 32]
-        g1s[c * 48 + 32 : c * 48 + 48] = gate_pair
-
-    copies = []
-    for k, (p, d) in enumerate(zc_peers):
-        copies.append(send(rows(g1s, p % 2, 48), rows(g1r, zc, 48), sg1, k, d))
-    rows(g1r, zc, 48)[...] = rows(g1s, core, 48)[...]
+    lane = iota((8, 128), 1)
+    gates[...] = jnp.where(lane == first, gate_a, 0.0) + jnp.where(lane == second, gate_b, 0.0)
+    g1s[...] = normed
+
+    copies = [
+        send(rows(g1s, p % 2, 32), rows(g1r, zc, 32), sg1, k, d) for k, (p, d) in enumerate(zc_peers)
+    ]
+    gate_copies = [
+        send(gates.at[pl.ds(0, 1)], gate_in.at[zc, pl.ds(0, 1)], sgate, k, d)
+        for k, (p, d) in enumerate(zc_peers)
+    ]
+    rows(g1r, zc, 32)[...] = rows(g1s, core, 32)[...]
+    gate_in[zc] = gates[...]
     for c in copies:
         c.wait_recv()
-    pending += copies
+    pending += copies + gate_copies
     g1f[...] = g1r[...].astype(F32)
     for j in range(16):
-        xa[core, y, x, :, j * 128 : j * 128 + 128] = g1f[pl.ds(j, 16, stride=48), :].astype(BF16)
-    for j in range(17):
-        xb[core, y, x, :, j * 128 : j * 128 + 128] = g1f[pl.ds(16 + j, 16, stride=48), :].astype(BF16)
-
-    first_a = [send(xa.at[core, y, x], xa.at[core, y, x], sg2, k, d) for k, (p, d) in enumerate(y_peers)]
-    first_b = [send(xb.at[core, y, x], xb.at[core, y, x], sg2, 3 + k, d) for k, (p, d) in enumerate(x_peers)]
-    for c in first_a + first_b:
-        c.wait_recv()
-    then_a = [send(xa.at[core, :, x], xa.at[core, :, x], sg3, k, d) for k, (p, d) in enumerate(x_peers)]
-    then_b = [send(xb.at[core, y], xb.at[core, y], sg3, 3 + k, d) for k, (p, d) in enumerate(y_peers)]
-    across = [
-        send(xa.at[core, :, x], xa.at[core, :, x], sg4, 0, sibling),
-        send(xb.at[core, y], xb.at[core, y], sg4, 4, sibling),
-    ]
-    for k in range(3):
-        from_x, from_y = (x + 3 - k) % 4, (y + 3 - k) % 4
-        then_a[k].wait_recv()
-        across.append(send(xa.at[core, :, from_x], xa.at[core, :, from_x], sg4, 1 + k, sibling))
-        then_b[k].wait_recv()
-        across.append(send(xb.at[core, from_y], xb.at[core, from_y], sg4, 5 + k, sibling))
-    pending += first_a + first_b + then_a + then_b + across
+        xa[core, y, x, :, j * 128 : j * 128 + 128] = g1f[pl.ds(j, 16, stride=32), :].astype(BF16)
+    for j in range(16):
+        xb[core, y, x, :, j * 128 : j * 128 + 128] = g1f[pl.ds(16 + j, 16, stride=32), :].astype(BF16)
+
+    def block(part, j, i):
+        if part == 0:
+            return xa.at[core, (y + 4 - j) % 4, (x + 4 - i) % 4]
+        return xb.at[core, (y + 4 - i) % 4, (x + 4 - j) % 4]
+
+    def line(part, i):
+        if part == 0:
+            return xa.at[core, :, (x + 4 - i) % 4]
+        return xb.at[core, (y + 4 - i) % 4]
+
+    first_axis = [[d for _, d in y_peers], [d for _, d in x_peers]]
+    second_axis = [[d for _, d in x_peers], [d for _, d in y_peers]]
+    across = []
+    middle = [[], []]
+    onward = [{}, {}]
+
+    def pass_on(part, j):
+        for to, k in ((0, 0), (2, 4)):
+            ref = block(part, j, 0)
+            onward[part][k + j] = send(ref, ref, sg3, part * 12 + k + j, second_axis[part][to])
+        ref = block(part, j, 0)
+        across.append(send(ref, ref, sg4, part * 7 + j, sibling))
+
+    def relay(part, j):
+        if j % 2 == 0:
+            onward[part][j].wait_recv()
+            ref, to = block(part, j, 1), second_axis[part][0]
+        else:
+            onward[part][4 + j].wait_recv()
+            ref, to = block(part, j, 3), second_axis[part][2]
+        onward[part][8 + j] = send(ref, ref, sg3, part * 12 + 8 + j, to)
+
+    for part in range(2):
+        ref = block(part, 0, 0)
+        for k in range(3):
+            middle[part].append(send(ref, ref, sg2, part * 3 + k, first_axis[part][k]))
+        pass_on(part, 0)
+    for j in (1, 3):
+        for part in range(2):
+            middle[part][j - 1].wait_recv()
+            pass_on(part, j)
+    for part in range(2):
+        relay(part, 0)
+    for part in range(2):
+        middle[part][1].wait_recv()
+        pass_on(part, 2)
+    for j in (1, 3, 2):
+        for part in range(2):
+            relay(part, j)
+    for c in gate_copies:
+        c.wait_recv()
+    for i in range(16):
+        gate_all[y, x, i : i + 1] = gate_in[i, 0:1]
+    ref = gate_all.at[y, x]
+    gate_middle = [send(ref, ref, sgate, 15 + k, d) for k, d in enumerate(first_axis[0])]
+    for part in range(2):
+        for j in (1, 3):
+            onward[part][j].wait_recv()
+        across.append(send(line(part, 1), line(part, 1), sg4, part * 7 + 4, sibling))
+        for j in (0, 2):
+            onward[part][4 + j].wait_recv()
+        across.append(send(line(part, 3), line(part, 3), sg4, part * 7 + 5, sibling))
+    for c in gate_middle:
+        c.wait_recv()
+    ref = gate_all.at[:, x]
+    gate_onward = [send(ref, ref, sgate, 18 + k, d) for k, d in enumerate(second_axis[0])]
+    for part in range(2):
+        for j in range(4):
+            onward[part][8 + j].wait_recv()
+        across.append(send(line(part, 2), line(part, 2), sg4, part * 7 + 6, sibling))
+    pending += across + gate_middle + gate_onward
+    for part in range(2):
+        pending += middle[part] + list(onward[part].values())
 
     for load in loads[2:]:
         load.wait()
@@ -304,78 +371,96 @@
     into(1 - core)
     gate_part = acc[0]
     act[...] = (gate_part / (1.0 + jnp.exp(-gate_part)) * acc[1]).astype(BF16)
-    pairs = xb[core, :, :, :, 2048:].reshape(256, 128).astype(F32)
-    mine = (iota((256, 128), 1) & 3) == tier
-    gate = jnp.sum(jnp.where(mine, pairs, 0.0), axis=1, keepdims=True)
-
-    def down(column):
+    for c in gate_onward:
+        c.wait_recv()
+    mine = iota((256, 128), 1) == tier
+    gate = jnp.sum(jnp.where(mine, gate_all[...].reshape(256, 128), 0.0), axis=1, keepdims=True)
+
+    def down(half, part, t):
+        column = pl.ds(pl.multiple_of(half * 4096 + part * 2048 + t * TN, TN), TN)
         return nn(act[...], w_down[:, column]) * gate
 
-    over = []
-    for part in range(2):
-        def tile(t, _, part=part):
-            at = pl.multiple_of(t * TN, TN)
-            column = pl.ds(pl.multiple_of((1 - core) * 4096 + part * 2048 + at, TN), TN)
-            f0s[part, :, :, :, pl.ds(at, TN)] = down(column).astype(BF16).reshape(4, 4, 16, TN)
-            return 0
-
-        lax.fori_loop(0, 2048 // TN, tile, 0)
-        over.append(send(f0s.at[part], f0r.at[part], sf0, part, sibling))
-    pending += over
-
-    then = []
-    for part in range(2):
-        over[part].wait_recv()
-
-        def tile(t, _, part=part):
-            at = pl.multiple_of(t * TN, TN)
-            column = pl.ds(pl.multiple_of(core * 4096 + part * 2048 + at, TN), TN)
-            both = down(column) + f0r[part, :, :, :, pl.ds(at, TN)].reshape(256, TN).astype(F32)
-            f1s[part, :, :, :, pl.ds(at, TN)] = both.astype(BF16).reshape(4, 4, 16, TN)
-            return 0
-
-        lax.fori_loop(0, 2048 // TN, tile, 0)
+    chunks = range(4)
+
+    def cut(t):
+        return slice(t * TN, t * TN + TN)
+
+    over = {}
+    for t in chunks:
+        for part in range(2):
+            f0s[part, :, :, :, cut(t)] = down(1 - core, part, t).astype(BF16).reshape(4, 4, 16, TN)
+            at = (part, slice(None), slice(None), slice(None), cut(t))
+            over[part, t] = send(f0s.at[at], f0r.at[at], sf0, part * 4 + t, sibling)
+
+    def toward(part, t, i):
         if part == 0:
-            then.append([send(f1s.at[0, :, p], f1ra.at[k], sf1, k, d) for k, (p, d) in enumerate(x_peers)])
-        else:
-            then.append([send(f1s.at[1, p], f1rb.at[k], sf1, 3 + k, d) for k, (p, d) in enumerate(y_peers)])
-    pending += then[0] + then[1]
-
-    last = []
-    for part in range(2):
-        for c in then[part]:
-            c.wait_recv()
-
-        def tile(t, _, part=part):
-            at = pl.ds(pl.multiple_of(t * TN, TN), TN)
-            if part == 0:
-                total = f1s[0, :, x, :, at].astype(F32)
+            return f1s.at[0, :, (x + 4 + i) % 4, :, cut(t)]
+        return f1s.at[1, (y + 4 + i) % 4, :, :, cut(t)]
+
+    plain, opposite, joined, final = {}, {}, {}, {}
+
+    def way(part, t):
+        axis = second_axis[part]
+        return (1, axis[0], axis[2]) if t % 2 == 0 else (-1, axis[2], axis[0])
+
+    def own_chunk(t):
+        for part in range(2):
+            over[part, t].wait_recv()
+            both = down(core, part, t) + f0r[part, :, :, :, cut(t)].reshape(256, TN).astype(F32)
+            f1s[part, :, :, :, cut(t)] = both.astype(BF16).reshape(4, 4, 16, TN)
+            step, ahead, behind = way(part, t)
+            k = (part * 4 + t) * 3
+            opposite[part, t] = send(toward(part, t, 2), fo.at[part, :, :, cut(t)], sf1, k, ahead)
+            plain[part, t] = send(toward(part, t, -step), fd.at[part, :, :, cut(t)], sf1, k + 1, behind)
+
+    def join_chunk(t):
+        for part in range(2):
+            step, ahead, behind = way(part, t)
+            opposite[part, t].wait_recv()
+            fcs[part, :, :, cut(t)] = (
+                toward(part, t, step)[...].astype(F32) + fo[part, :, :, cut(t)].astype(F32)
+            ).astype(BF16)
+            at = (part, slice(None), slice(None), cut(t))
+            joined[part, t] = send(fcs.at[at], fcr.at[at], sf1, (part * 4 + t) * 3 + 2, ahead)
+
+    def end_chunk(t):
+        for part in range(2):
+            plain[part, t].wait_recv()
+            joined[part, t].wait_recv()
+            f2s[part, :, :, cut(t)] = (
+                toward(part, t, 0)[...].astype(F32)
+                + fd[part, :, :, cut(t)].astype(F32)
+                + fcr[part, :, :, cut(t)].astype(F32)
+            ).astype(BF16)
+            for k, (p, d) in enumerate((y_peers, x_peers)[part]):
+                final[part, t, k] = send(
+                    f2s.at[part, p, :, cut(t)], f2r.at[part, k, :, cut(t)], sf2, (part * 4 + t) * 3 + k, d
+                )
+
+    own_chunk(0)
+    own_chunk(1)
+    join_chunk(0)
+    own_chunk(2)
+    join_chunk(1)
+    own_chunk(3)
+    join_chunk(2)
+    end_chunk(0)
+    join_chunk(3)
+    end_chunk(1)
+    end_chunk(2)
+    end_chunk(3)
+    for sent in (over, plain, opposite, joined, final):
+        pending += list(sent.values())
+    for t in chunks:
+        for part in range(2):
+            for k in range(3):
+                final[part, t, k].wait_recv()
+            for j in range(t * 4, t * 4 + 4):
+                at = slice(j * 128, j * 128 + 128)
+                total = f2s[part, (y, x)[part], :, at].astype(F32)
                 for k in range(3):
-                    total = total + f1ra[k, :, :, at].astype(F32)
-                f2sa[:, :, at] = total.astype(BF16)
-            else:
-                total = f1s[1, y, :, :, at].astype(F32)
-                for k in range(3):
-                    total = total + f1rb[k, :, :, at].astype(F32)
-                f2sb[:, :, at] = total.astype(BF16)
-            return 0
-
-        lax.fori_loop(0, 2048 // TN, tile, 0)
-        if part == 0:
-            last.append([send(f2sa.at[p], f2ra.at[k], sf2, k, d) for k, (p, d) in enumerate(y_peers)])
-        else:
-            last.append([send(f2sb.at[p], f2rb.at[k], sf2, 3 + k, d) for k, (p, d) in enumerate(x_peers)])
-    pending += last[0] + last[1]
-    for c in last[0] + last[1]:
-        c.wait_recv()
-    for j in range(16):
-        at = slice(j * 128, j * 128 + 128)
-        total_a, total_b = f2sa[y, :, at].astype(F32), f2sb[x, :, at].astype(F32)
-        for k in range(3):
-            total_a = total_a + f2ra[k, :, at].astype(F32)
-            total_b = total_b + f2rb[k, :, at].astype(F32)
-        f3f[pl.ds(j, 16, stride=32), :] = total_a
-        f3f[pl.ds(16 + j, 16, stride=32), :] = total_b
+                    total = total + f2r[part, k, :, at].astype(F32)
+                f3f[pl.ds(part * 16 + j, 16, stride=32), :] = total
     f3s[...] = f3f[...].astype(BF16)
     copies = [send(rows(f3s, p, 32), f3r.at[zc], sf3, k, d) for k, (p, d) in enumerate(zc_peers)]
     f3r[zc] = rows(f3s, zc, 32)[...]
@@ -414,23 +499,25 @@
             v((64, 128), F32), v((64, 128), F32), v((64, 128), F32), v((64, 128), F32),
             v((8, 16, CZ // 2), BF16), v((7, 16, CZ // 2), BF16),
             v((8, 16, CX // 2), BF16), v((7, 16, CX // 2), BF16),
-            v((8 * SZ, 128), F32), v((7, SZ, 128), F32), v((8 * SX, 128), F32), v((7, SX, 128), F32),
-            v((64, 128), F32), v((96, 128), BF16), v((768, 128), BF16), v((768, 128), F32),
-            v((2, 4, 4, 16, 2048), BF16), v((2, 4, 4, 16, 2176), BF16),
+            v((8 * PZ, 128), BF16), v((7, PZ, 128), BF16), v((8 * PX, 128), BF16), v((7, PX, 128), BF16),
+            v((8 * PZ, 128), F32), v((8 * PX, 128), F32), v((64, 128), F32), v((256, 128), F32),
+            v((64, 128), BF16), v((512, 128), BF16), v((512, 128), F32),
+            v((8, 128), F32), v((16, 8, 128), F32), v((4, 4, 16, 128), F32),
+            v((2, 4, 4, 16, 2048), BF16), v((2, 4, 4, 16, 2048), BF16),
             v((2, 256, 192), F32), v((256, 192), BF16),
             v((2, 4, 4, 16, 2048), BF16), v((2, 4, 4, 16, 2048), BF16), v((2, 4, 4, 16, 2048), BF16),
-            v((3, 4, 16, 2048), BF16), v((3, 4, 16, 2048), BF16),
-            v((4, 16, 2048), BF16), v((4, 16, 2048), BF16), v((3, 16, 2048), BF16), v((3, 16, 2048), BF16),
+            v((2, 4, 16, 2048), BF16), v((2, 4, 16, 2048), BF16), v((2, 4, 16, 2048), BF16), v((2, 4, 16, 2048), BF16),
+            v((2, 4, 16, 2048), BF16), v((2, 3, 16, 2048), BF16),
             v((512, 128), F32), v((512, 128), BF16), v((16, 32, 128), BF16),
             sem(7), sem(7), sem(7), sem(7), sem(7), sem(7), sem(7), sem(7),
-            sem(15), sem(6), sem(6), sem(8), sem(2), sem(6), sem(6), sem(15),
+            sem(15), sem(21), sem(6), sem(24), sem(14), sem(8), sem(24), sem(24), sem(15),
         ],
         compiler_params=pltpu.CompilerParams(
             collective_id=0, has_side_effects=True, vmem_limit_bytes=60 * 2**20
         ),
     )(
-        cache_home, cached_len, expert_ids, query, fresh_kv, resid.reshape(64, 128),
-        norm_gain.reshape(64, 128), jnp.transpose(w_router).reshape(4, 64, 128),
+        cache_home, cached_len, expert_ids, query, jnp.transpose(fresh_kv), resid,
+        norm_gain.reshape(64, 128), jnp.transpose(w_router),
         kv_cache, wo, w_gate, w_up, w_down,
     )
     return out.reshape(1, 8192)

time: 120 us -> 109 us (0.908)
  Pallas kernels: 113 us -> 107 us
  local copies, waits for them, and re-layouts: 4.21 us -> 1.36 us
  other arithmetic: 1.45 us -> 0 us
    pallas_call x1, Pallas kernels: 113 us -> 107 us  [on_device(): pl.pallas_call(kernel, out_shape=jax.ShapeDtypeStruct((64, 128), BF16), i...]
    unnamed x3 -> x1, local copies, waits for them, and re-layouts: 4.21 us -> 1.36 us
    unnamed x1 -> x0, other arithmetic: 1.45 us -> none
where the time goes in v2:
time: 109 us
  Pallas kernels  107 us (98%)
  local copies, waits for them, and re-layouts  1.36 us (1%)
    pallas_call x1, Pallas kernels, on_device(): pl.pallas_call(kernel, out_shape=jax.ShapeDtypeStruct((64, 128), BF16), i...  107 us

profile of v2, /device:TPU:1, one launch (start us, length us, event | category | flops | bytes accessed | tf_op | source)
XLA Modules:
  0.0 109.0 jit_solution(9041136498714469595)
XLA Ops:
  0.7 106.9 %shard_map.127 = bf16[64,128]{1,0:T(8,128)(2,1)} custom-call(s32[1,64]{1,0:T(1,128)} %home_ref.1, s32[1]{0:T(128)S(6)} %copy.17.len_ref, s32[1,2]{1,0:T(1,128)} %ids_ref.1, bf16[64,128]{1,0:T(8,128)(2,1)} %query_ref.1, bf16[32,64]{1,0:T(8,128)(2,1)} %bitcast.11, bf16[1,8192]{1,0:T(2,128)(2,1)} %resid_ref.1, bf16[64,128]{1,0:T(8,128)(2,1)} %bitcast.10, ...), custom_call_target="tpu_custom_call" | custom-call | tf_op jit(solution)/shard_map/pallas_call | solution.py:490
  107.6 1.4 %copy.16 = bf16[1,1,64,128]{3,1,2,0:T(2,128)(2,1)} copy(bf16[1,1,64,128]{3,2,1,0:T(8,128)(2,1)} %bitcast.9) | data formatting | bytes 32768

commit v3 on v2

--- a/solution.py
+++ b/solution.py
@@ -32,11 +32,11 @@
 
 
 def kernel(
-    home_ref, len_ref, ids_ref, query_ref, fresh_ref, resid_ref, gain_ref, router_ref,
+    home_ref, len_ref, ids_ref, query_ref, fresh_ref, resid_hbm, gain_hbm, router_hbm,
     cache_hbm, wo_hbm, gate_hbm, up_hbm, down_hbm,
     out_ref,
     cache, wo, w_in, w_down, local_sem,
-    a1s, a1r, a2s, a2r, c1s, c1r, c2s, c2r,
+    resid, gain, router_in, a1s, a1r, a1f, a2s, a2r, c1s, c1r, c2s, c2r,
     r1zs, r1zr, r1xs, r1xr, r2zs, r2zr, r2xs, r2xr,
     r2fz, r2fx, hid, router,
     g1s, g1r, g1f, gates, gate_in, gate_all, xa, xb, acc, act,
@@ -61,15 +61,18 @@
         copy.start()
         return copy
 
-    z_peers = [((z + k) % 8, device(y, (z + k) % 8, x, core)) for k in range(1, 8)]
+    far_first = (4, 3, 5, 2, 6, 1, 7)
+    z_peers = [((z + k) % 8, device(y, (z + k) % 8, x, core)) for k in far_first]
     xy_peers = []
-    for k in range(1, 8):
-        px, pl_lo = (x + k) % 4, (y_lo + k // 4) % 2
-        xy_peers.append((pl_lo * 4 + px, device(y_hi * 2 + pl_lo, z, px, core)))
+    for k_lo, k in ((1, 2), (0, 2), (1, 1), (1, 3), (0, 1), (0, 3), (1, 0)):
+        px, p_lo = (x + k) % 4, (y_lo + k_lo) % 2
+        xy_peers.append((p_lo * 4 + px, device(y_hi * 2 + p_lo, z, px, core)))
     zc_peers = []
-    for k in range(1, 16):
-        pz, pc = (z + k // 2) % 8, (core + k % 2) % 2
-        zc_peers.append((pz * 2 + pc, device(y, pz, x, pc)))
+    for k in far_first + (0,):
+        for k_core in (1, 0)[: 2 if k else 1]:
+            pz, pc = (z + k) % 8, (core + k_core) % 2
+            zc_peers.append((pz * 2 + pc, device(y, pz, x, pc)))
+
     x_peers = [((x + k) % 4, device(y, z, (x + k) % 4, core)) for k in range(1, 4)]
     y_peers = [((y + k) % 4, device((y + k) % 4, z, x, core)) for k in range(1, 4)]
     sibling = device(y, z, x, 1 - core)
@@ -81,10 +84,10 @@
         pltpu.make_async_copy(gate_hbm.at[0], w_in.at[0], local_sem.at[2]),
         pltpu.make_async_copy(up_hbm.at[0], w_in.at[1], local_sem.at[3]),
         pltpu.make_async_copy(down_hbm.at[0], w_down, local_sem.at[4]),
-    ]
-    for load in loads:
-        load.start()
-
+        pltpu.make_async_copy(resid_hbm, resid, local_sem.at[5]),
+        pltpu.make_async_copy(gain_hbm, gain, local_sem.at[6]),
+        pltpu.make_async_copy(router_hbm, router_in, local_sem.at[7]),
+    ]
     barrier = pltpu.get_barrier_semaphore()
     greeted = [d for _, d in zc_peers] + [d for _, d in xy_peers] + far
     for d in greeted:
@@ -97,43 +100,49 @@
     by_slot_q = nn(to_slot, query_ref[...])
     by_slot_f = nn(nt(to_slot, fresh_ref[...]).astype(BF16), spread_fresh)
     for k in range(8):
-        a1s[k * 16 : k * 16 + 8] = by_slot_q[k * 8 : k * 8 + 8]
-        a1s[k * 16 + 8 : k * 16 + 16] = by_slot_f[k * 8 : k * 8 + 8]
-
-    resid_row, router_rows = resid_ref[...].astype(F32), router_ref[...].astype(F32)
+        a1s[k * 16 : k * 16 + 16] = jnp.concatenate(
+            [by_slot_q[k * 8 : k * 8 + 8], by_slot_f[k * 8 : k * 8 + 8]], axis=0
+        ).astype(BF16)
+
+    pl.semaphore_wait(barrier, len(greeted))
+
+    def rows(ref, i, n):
+        return ref.at[pl.ds(pl.multiple_of(i * n, n), n)]
+
+    pending = []
+    copies = [
+        send(rows(a1s, p, 16), rows(a1r, z, 16), sa1, k, d) for k, (p, d) in enumerate(z_peers)
+    ]
+    rows(a1r, z, 16)[...] = rows(a1s, z, 16)[...]
+    for load in loads[5:] + loads[:5]:
+        load.start()
+    r2fz[...] = jnp.zeros_like(r2fz)
+    r2fx[...] = jnp.zeros_like(r2fx)
+    for c in copies:
+        c.wait_recv()
+    pending += copies
+    a1f[...] = a1r[...].astype(F32)
+    for k in range(8):
+        a2s[k * 16 : k * 16 + 16] = jnp.concatenate(
+            [a1f[pl.ds(k, 8, stride=16), :], a1f[pl.ds(8 + k, 8, stride=16), :]], axis=0
+        ).astype(BF16)
+    copies = [
+        send(rows(a2s, p, 16), rows(a2r, xy, 16), sa2, k, d) for k, (p, d) in enumerate(xy_peers)
+    ]
+    rows(a2r, xy, 16)[...] = rows(a2s, xy, 16)[...]
+    for load in loads[5:]:
+        load.wait()
+    resid_row, router_rows = resid[...].astype(F32), router_in[...].astype(F32)
     for j in range(64):
         hid[j : j + 1] = resid_row[:, j * 128 : j * 128 + 128]
         router[pl.ds(j, 4, stride=64), :] = router_rows[:, j * 128 : j * 128 + 128]
-    r2fz[...] = jnp.zeros_like(r2fz)
-    r2fx[...] = jnp.zeros_like(r2fx)
-
-    pl.semaphore_wait(barrier, len(greeted))
-
-    def rows(ref, i, n):
-        return ref.at[pl.ds(pl.multiple_of(i * n, n), n)]
-
-    pending = []
-    copies = [
-        send(rows(a1s, p, 16), rows(a1r, z, 16), sa1, k, d) for k, (p, d) in enumerate(z_peers)
-    ]
-    rows(a1r, z, 16)[...] = rows(a1s, z, 16)[...]
-    for c in copies:
-        c.wait_recv()
-    pending += copies
-    for k in range(8):
-        for half in range(2):
-            a2s[k * 16 + half * 8 : k * 16 + half * 8 + 8] = a1r[pl.ds(half * 8 + k, 8, stride=16), :]
-    copies = [
-        send(rows(a2s, p, 16), rows(a2r, xy, 16), sa2, k, d) for k, (p, d) in enumerate(xy_peers)
-    ]
-    rows(a2r, xy, 16)[...] = rows(a2s, xy, 16)[...]
     for c in copies:
         c.wait_recv()
     pending += copies
 
     head = iota((64, 128), 0)
     group = (head >> 5) * 4 + ((head & 7) >> 1)
-    got = a2r[...].reshape(8, 16, 128)
+    got = a2r[...].astype(F32).reshape(8, 16, 128)
     queries = got[:, :8].reshape(64, 128)
     news = got[:, 8:]
     new_key = (news[0] + news[1] + news[2] + news[3]).astype(BF16)
@@ -240,7 +249,7 @@
     hid[...] = hidden
 
     mean = jnp.sum(hidden * hidden, keepdims=True) * (1.0 / 8192)
-    normed = (hidden * lax.rsqrt(mean + 1e-05) * gain_ref[...].astype(F32)).astype(BF16)
+    normed = (hidden * lax.rsqrt(mean + 1e-05) * gain[...].astype(F32)).astype(BF16)
     normed_wide = normed.astype(F32)
     logits = [
         jnp.sum(normed_wide * router[e * 64 : e * 64 + 64], keepdims=True) for e in range(4)
@@ -257,23 +266,21 @@
     gates[...] = jnp.where(lane == first, gate_a, 0.0) + jnp.where(lane == second, gate_b, 0.0)
     g1s[...] = normed
 
-    copies = [
-        send(rows(g1s, p % 2, 32), rows(g1r, zc, 32), sg1, k, d) for k, (p, d) in enumerate(zc_peers)
+    halves = [
+        [
+            send(rows(g1s, p % 2 * 2 + part, 16), rows(g1r, part * 16 + zc, 16), sg1, part * 15 + k, d)
+            for k, (p, d) in enumerate(zc_peers)
+        ]
+        for part in range(2)
     ]
     gate_copies = [
         send(gates.at[pl.ds(0, 1)], gate_in.at[zc, pl.ds(0, 1)], sgate, k, d)
         for k, (p, d) in enumerate(zc_peers)
     ]
-    rows(g1r, zc, 32)[...] = rows(g1s, core, 32)[...]
+    for part in range(2):
+        rows(g1r, part * 16 + zc, 16)[...] = rows(g1s, core * 2 + part, 16)[...]
     gate_in[zc] = gates[...]
-    for c in copies:
-        c.wait_recv()
-    pending += copies + gate_copies
-    g1f[...] = g1r[...].astype(F32)
-    for j in range(16):
-        xa[core, y, x, :, j * 128 : j * 128 + 128] = g1f[pl.ds(j, 16, stride=32), :].astype(BF16)
-    for j in range(16):
-        xb[core, y, x, :, j * 128 : j * 128 + 128] = g1f[pl.ds(16 + j, 16, stride=32), :].astype(BF16)
+    pending += halves[0] + halves[1] + gate_copies
 
     def block(part, j, i):
         if part == 0:
@@ -288,15 +295,16 @@
     first_axis = [[d for _, d in y_peers], [d for _, d in x_peers]]
     second_axis = [[d for _, d in x_peers], [d for _, d in y_peers]]
     across = []
-    middle = [[], []]
+    middle = [{}, {}]
     onward = [{}, {}]
 
     def pass_on(part, j):
+        ref = block(part, j, 0)
         for to, k in ((0, 0), (2, 4)):
-            ref = block(part, j, 0)
             onward[part][k + j] = send(ref, ref, sg3, part * 12 + k + j, second_axis[part][to])
-        ref = block(part, j, 0)
-        across.append(send(ref, ref, sg4, part * 7 + j, sibling))
+        if j == 2:
+            onward[part][10] = send(ref, ref, sg3, part * 12 + 10, second_axis[part][1])
+        across.append(send(ref, ref, sg4, part * 10 + j, sibling))
 
     def relay(part, j):
         if j % 2 == 0:
@@ -308,9 +316,14 @@
         onward[part][8 + j] = send(ref, ref, sg3, part * 12 + 8 + j, to)
 
     for part in range(2):
+        for c in halves[part]:
+            c.wait_recv()
+        g1f[...] = rows(g1r, part, 256)[...].astype(F32)
+        for j in range(16):
+            block(part, 0, 0)[:, j * 128 : j * 128 + 128] = g1f[pl.ds(j, 16, stride=16), :].astype(BF16)
         ref = block(part, 0, 0)
-        for k in range(3):
-            middle[part].append(send(ref, ref, sg2, part * 3 + k, first_axis[part][k]))
+        for k in (1, 0, 2):
+            middle[part][k] = send(ref, ref, sg2, part * 3 + k, first_axis[part][k])
         pass_on(part, 0)
     for j in (1, 3):
         for part in range(2):
@@ -321,7 +334,7 @@
     for part in range(2):
         middle[part][1].wait_recv()
         pass_on(part, 2)
-    for j in (1, 3, 2):
+    for j in (1, 3):
         for part in range(2):
             relay(part, j)
     for c in gate_copies:
@@ -331,25 +344,25 @@
     ref = gate_all.at[y, x]
     gate_middle = [send(ref, ref, sgate, 15 + k, d) for k, d in enumerate(first_axis[0])]
     for part in range(2):
-        for j in (1, 3):
+        for j in (1, 2, 3):
             onward[part][j].wait_recv()
-        across.append(send(line(part, 1), line(part, 1), sg4, part * 7 + 4, sibling))
+        across.append(send(line(part, 1), line(part, 1), sg4, part * 10 + 4, sibling))
         for j in (0, 2):
             onward[part][4 + j].wait_recv()
-        across.append(send(line(part, 3), line(part, 3), sg4, part * 7 + 5, sibling))
+        across.append(send(line(part, 3), line(part, 3), sg4, part * 10 + 5, sibling))
     for c in gate_middle:
         c.wait_recv()
     ref = gate_all.at[:, x]
     gate_onward = [send(ref, ref, sgate, 18 + k, d) for k, d in enumerate(second_axis[0])]
     for part in range(2):
-        for j in range(4):
+        for j in (0, 1, 3, 2):
             onward[part][8 + j].wait_recv()
-        across.append(send(line(part, 2), line(part, 2), sg4, part * 7 + 6, sibling))
+            across.append(send(block(part, j, 2), block(part, j, 2), sg4, part * 10 + 6 + j, sibling))
     pending += across + gate_middle + gate_onward
     for part in range(2):
-        pending += middle[part] + list(onward[part].values())
-
-    for load in loads[2:]:
+        pending += list(middle[part].values()) + list(onward[part].values())
+
+    for load in loads[2:5]:
         load.wait()
     acc[...] = jnp.zeros_like(acc)
 
@@ -410,6 +423,13 @@
             f1s[part, :, :, :, cut(t)] = both.astype(BF16).reshape(4, 4, 16, TN)
             step, ahead, behind = way(part, t)
             k = (part * 4 + t) * 3
+            if t == 3:
+                axis = second_axis[part]
+                at = (part, slice(None), slice(None), cut(t))
+                opposite[part, t] = send(toward(part, t, 2), fo.at[at], sf1, k, axis[1])
+                plain[part, t] = send(toward(part, t, 1), fd.at[at], sf1, k + 1, axis[0])
+                joined[part, t] = send(toward(part, t, 3), fcr.at[at], sf1, k + 2, axis[2])
+                continue
             opposite[part, t] = send(toward(part, t, 2), fo.at[part, :, :, cut(t)], sf1, k, ahead)
             plain[part, t] = send(toward(part, t, -step), fd.at[part, :, :, cut(t)], sf1, k + 1, behind)
 
@@ -427,15 +447,38 @@
         for part in range(2):
             plain[part, t].wait_recv()
             joined[part, t].wait_recv()
-            f2s[part, :, :, cut(t)] = (
+            total = (
                 toward(part, t, 0)[...].astype(F32)
                 + fd[part, :, :, cut(t)].astype(F32)
                 + fcr[part, :, :, cut(t)].astype(F32)
-            ).astype(BF16)
+            )
+            if t == 3:
+                opposite[part, t].wait_recv()
+                total = total + fo[part, :, :, cut(t)].astype(F32)
+            f2s[part, :, :, cut(t)] = total.astype(BF16)
             for k, (p, d) in enumerate((y_peers, x_peers)[part]):
                 final[part, t, k] = send(
                     f2s.at[part, p, :, cut(t)], f2r.at[part, k, :, cut(t)], sf2, (part * 4 + t) * 3 + k, d
                 )
+
+    last = {}
+
+    def finish_chunk(t):
+        half = t // 2
+        for part in range(2):
+            for k in range(3):
+                final[part, t, k].wait_recv()
+            for j in range(4):
+                at = slice((t * 4 + j) * 128, (t * 4 + j + 1) * 128)
+                total = f2s[part, (y, x)[part], :, at].astype(F32)
+                for k in range(3):
+                    total = total + f2r[part, k, :, at].astype(F32)
+                f3f[pl.ds(half * 256 + part * 8 + t % 2 * 4 + j, 16, stride=16), :] = total
+        if t % 2 == 1:
+            rows(f3s, half, 256)[...] = rows(f3f, half, 256)[...].astype(BF16)
+            for k, (p, d) in enumerate(zc_peers):
+                last[half, k] = send(rows(f3s, half * 16 + p, 16), f3r.at[half, zc], sf3, half * 15 + k, d)
+            f3r[half, zc] = rows(f3s, half * 16 + zc, 16)[...]
 
     own_chunk(0)
     own_chunk(1)
@@ -445,33 +488,27 @@
     own_chunk(3)
     join_chunk(2)
     end_chunk(0)
-    join_chunk(3)
     end_chunk(1)
     end_chunk(2)
+    finish_chunk(0)
     end_chunk(3)
-    for sent in (over, plain, opposite, joined, final):
+    finish_chunk(1)
+    finish_chunk(2)
+    finish_chunk(3)
+    for sent in (over, plain, opposite, joined, final, last):
         pending += list(sent.values())
-    for t in chunks:
-        for part in range(2):
-            for k in range(3):
-                final[part, t, k].wait_recv()
-            for j in range(t * 4, t * 4 + 4):
-                at = slice(j * 128, j * 128 + 128)
-                total = f2s[part, (y, x)[part], :, at].astype(F32)
-                for k in range(3):
-                    total = total + f2r[part, k, :, at].astype(F32)
-                f3f[pl.ds(part * 16 + j, 16, stride=32), :] = total
-    f3s[...] = f3f[...].astype(BF16)
-    copies = [send(rows(f3s, p, 32), f3r.at[zc], sf3, k, d) for k, (p, d) in enumerate(zc_peers)]
-    f3r[zc] = rows(f3s, zc, 32)[...]
-    for c in copies:
-        c.wait_recv()
-    pending += copies
-    low, high = f3r[0].astype(F32), f3r[1].astype(F32)
-    for k in range(1, 8):
-        low = low + f3r[2 * k].astype(F32)
-        high = high + f3r[2 * k + 1].astype(F32)
-    out_ref[...] = (hid[...] + jnp.concatenate([low, high], axis=0)).astype(BF16)
+    for c in last.values():
+        c.wait_recv()
+    sums = []
+    for c in range(2):
+        parts = []
+        for half in range(2):
+            total = f3r[half, c].astype(F32)
+            for k in range(1, 8):
+                total = total + f3r[half, 2 * k + c].astype(F32)
+            parts.append(total)
+        sums += [parts[0][:8], parts[1][:8], parts[0][8:], parts[1][8:]]
+    out_ref[...] = (hid[...] + jnp.concatenate(sums, axis=0)).astype(BF16)
     for c in pending:
         c.wait_send()
 
@@ -490,27 +527,28 @@
     out = pl.pallas_call(
         kernel,
         out_shape=jax.ShapeDtypeStruct((64, 128), BF16),
-        in_specs=[vmem, smem, smem, vmem, vmem, vmem, vmem, vmem, hbm, hbm, hbm, hbm, hbm],
+        in_specs=[vmem, smem, smem, vmem, vmem] + [hbm] * 8,
         out_specs=vmem,
         scratch_shapes=[
             v((128, 2048), BF16), v((128, 8192), BF16), v((2, 192, 8192), BF16), v((192, 8192), BF16),
-            pltpu.SemaphoreType.DMA((5,)),
-            v((128, 128), F32), v((128, 128), F32), v((128, 128), F32), v((128, 128), F32),
+            pltpu.SemaphoreType.DMA((8,)),
+            v((1, 8192), BF16), v((64, 128), BF16), v((4, 8192), BF16),
+            v((128, 128), BF16), v((128, 128), BF16), v((128, 128), F32), v((128, 128), BF16), v((128, 128), BF16),
             v((64, 128), F32), v((64, 128), F32), v((64, 128), F32), v((64, 128), F32),
             v((8, 16, CZ // 2), BF16), v((7, 16, CZ // 2), BF16),
             v((8, 16, CX // 2), BF16), v((7, 16, CX // 2), BF16),
             v((8 * PZ, 128), BF16), v((7, PZ, 128), BF16), v((8 * PX, 128), BF16), v((7, PX, 128), BF16),
             v((8 * PZ, 128), F32), v((8 * PX, 128), F32), v((64, 128), F32), v((256, 128), F32),
-            v((64, 128), BF16), v((512, 128), BF16), v((512, 128), F32),
+            v((64, 128), BF16), v((512, 128), BF16), v((256, 128), F32),
             v((8, 128), F32), v((16, 8, 128), F32), v((4, 4, 16, 128), F32),
             v((2, 4, 4, 16, 2048), BF16), v((2, 4, 4, 16, 2048), BF16),
             v((2, 256, 192), F32), v((256, 192), BF16),
             v((2, 4, 4, 16, 2048), BF16), v((2, 4, 4, 16, 2048), BF16), v((2, 4, 4, 16, 2048), BF16),
             v((2, 4, 16, 2048), BF16), v((2, 4, 16, 2048), BF16), v((2, 4, 16, 2048), BF16), v((2, 4, 16, 2048), BF16),
             v((2, 4, 16, 2048), BF16), v((2, 3, 16, 2048), BF16),
-            v((512, 128), F32), v((512, 128), BF16), v((16, 32, 128), BF16),
+            v((512, 128), F32), v((512, 128), BF16), v((2, 16, 16, 128), BF16),
             sem(7), sem(7), sem(7), sem(7), sem(7), sem(7), sem(7), sem(7),
-            sem(15), sem(21), sem(6), sem(24), sem(14), sem(8), sem(24), sem(24), sem(15),
+            sem(30), sem(21), sem(6), sem(24), sem(20), sem(8), sem(24), sem(24), sem(30),
         ],
         compiler_params=pltpu.CompilerParams(
             collective_id=0, has_side_effects=True, vmem_limit_bytes=60 * 2**20

time: 109 us -> 104 us (0.954)
  Pallas kernels: 107 us -> 102 us
    pallas_call x1, Pallas kernels: 107 us -> 102 us  [on_device(): pl.pallas_call(kernel, out_shape=jax.ShapeDtypeStruct((64, 128), BF16), i...]
where the time goes in v3:
time: 104 us
  Pallas kernels  102 us (98%)
  local copies, waits for them, and re-layouts  1.36 us (1%)
    pallas_call x1, Pallas kernels, on_device(): pl.pallas_call(kernel, out_shape=jax.ShapeDtypeStruct((64, 128), BF16), i...  102 us

profile of v3, /device:TPU:1, one launch (start us, length us, event | category | flops | bytes accessed | tf_op | source)
XLA Modules:
  0.0 103.7 jit_solution(3531504926043008357)
XLA Ops:
  0.7 101.7 %shard_map.127 = bf16[64,128]{1,0:T(8,128)(2,1)} custom-call(s32[1,64]{1,0:T(1,128)} %home_ref.1, s32[1]{0:T(128)S(6)} %copy.17.len_ref, s32[1,2]{1,0:T(1,128)} %ids_ref.1, bf16[64,128]{1,0:T(8,128)(2,1)} %query_ref.1, bf16[32,64]{1,0:T(8,128)(2,1)} %bitcast.11, bf16[1,8192]{1,0:T(2,128)(2,1)} %resid_hbm.1, bf16[64,128]{1,0:T(8,128)(2,1)} %bitcast.10, ...), custom_call_target="tpu_custom_call" | custom-call | tf_op jit(solution)/shard_map/pallas_call | solution.py:527
  102.3 1.4 %copy.16 = bf16[1,1,64,128]{3,1,2,0:T(2,128)(2,1)} copy(bf16[1,1,64,128]{3,2,1,0:T(8,128)(2,1)} %bitcast.9) | data formatting | bytes 32768

commit v4 on v3

--- a/solution.py
+++ b/solution.py
@@ -11,10 +11,9 @@
 MESH = pl.DeviceIdType.MESH
 F32 = jnp.float32
 BF16 = jnp.bfloat16
-CZ = 3072
-CX = 8192 - CZ
-SZ = CZ // 128
-SX = CX // 128
+WZ = 768
+WX = 2048 - WZ
+SZ, SX = 2 * WZ // 128, 2 * WX // 128
 PZ, PX = -(-SZ // 16) * 16, -(-SX // 16) * 16
 TN = 512
 
@@ -197,63 +196,87 @@
     loads[1].wait()
 
     def project(att, ref, base, width):
-        def tile(t, _):
-            at = pl.multiple_of(t * TN, TN)
-            lo = nn(att, wo[:, pl.ds(base + at, TN)]).reshape(8, 8, TN)
-            hi = nn(att, wo[:, pl.ds(base + width + at, TN)]).reshape(8, 8, TN)
-            ref[:, :, pl.ds(at, TN)] = jnp.concatenate([lo, hi], axis=1).astype(BF16)
-            return 0
-
-        lax.fori_loop(0, width // TN, tile, 0)
-
-    project(att_z, r1zs, 0, CZ // 2)
-    copies_z = [send(r1zs.at[p], r1zr.at[k], sr1z, k, d) for k, (p, d) in enumerate(z_peers)]
-    project(att_x, r1xs, CZ, CX // 2)
-    copies_x = [send(r1xs.at[p], r1xr.at[k], sr1x, k, d) for k, (p, d) in enumerate(xy_peers)]
-    pending += copies_z + copies_x
-
-    def fold(sent, mine, received, n, slabs, used, stride):
-        def tile(j, _):
-            at = pl.multiple_of(j * 128, 128)
-            total = sent[mine, :, pl.ds(at, 128)].astype(F32)
-            for k in range(n):
-                total = total + received[k, :, pl.ds(at, 128)].astype(F32)
-            slabs[pl.ds(j, 8, stride=stride), :] = total[:8]
-            slabs[pl.ds(j + used // 2, 8, stride=stride), :] = total[8:]
-            return 0
-
-        lax.fori_loop(0, used // 2, tile, 0)
-
-    for c in copies_z:
-        c.wait_recv()
-    fold(r1zs, z, r1zr, 7, r2fz, SZ, PZ)
-    r2zs[...] = r2fz[...].astype(BF16)
-    copies_z = [
-        send(rows(r2zs, p, PZ), r2zr.at[k], sr2z, k, d) for k, (p, d) in enumerate(xy_peers)
-    ]
-    for c in copies_x:
-        c.wait_recv()
-    fold(r1xs, xy, r1xr, 7, r2fx, SX, PX)
-    r2xs[...] = r2fx[...].astype(BF16)
-    copies_x = [
-        send(rows(r2xs, p, PX), r2xr.at[k], sr2x, k, d) for k, (p, d) in enumerate(z_peers)
-    ]
-    for c in copies_z + copies_x:
-        c.wait_recv()
-    pending += copies_z + copies_x
-    part_z, part_x = rows(r2fz, xy, PZ)[...], rows(r2fx, z, PX)[...]
-    for k in range(7):
-        part_z = part_z + r2zr[k].astype(F32)
-        part_x = part_x + r2xr[k].astype(F32)
-    hidden = hid[...] + jnp.concatenate([part_z[:SZ], part_x[:SX]], axis=0)
-    hid[...] = hidden
-
-    mean = jnp.sum(hidden * hidden, keepdims=True) * (1.0 / 8192)
-    normed = (hidden * lax.rsqrt(mean + 1e-05) * gain[...].astype(F32)).astype(BF16)
-    normed_wide = normed.astype(F32)
-    logits = [
-        jnp.sum(normed_wide * router[e * 64 : e * 64 + 64], keepdims=True) for e in range(4)
-    ]
+        for at in range(0, width, width // 2):
+            cut = slice(at, at + width // 2)
+            lo = nn(att, wo[:, base + at : base + at + width // 2]).reshape(8, 8, width // 2)
+            hi = nn(att, wo[:, 4096 + base + at : 4096 + base + at + width // 2]).reshape(8, 8, width // 2)
+            ref[:, :, cut] = jnp.concatenate([lo, hi], axis=1).astype(BF16)
+
+    def fold(sent, mine, received, slabs, base, used, stride):
+        for j in range(used // 2):
+            at = slice(j * 128, j * 128 + 128)
+            total = sent[mine, :, at].astype(F32)
+            for k in range(7):
+                total = total + received[k, :, at].astype(F32)
+            slabs[pl.ds(base + j, 8, stride=stride), :] = total[:8]
+            slabs[pl.ds(base + j + used // 2, 8, stride=stride), :] = total[8:]
+
+    copies_z, copies_x = [], []
+    for part in range(2):
+        project(att_z, r1zs.at[part], part * 2048, WZ)
+        copies_z.append([
+            send(r1zs.at[part, p], r1zr.at[part, k], sr1z, part * 7 + k, d) for k, (p, d) in enumerate(z_peers)
+        ])
+        project(att_x, r1xs.at[part], part * 2048 + WZ, WX)
+        copies_x.append([
+            send(r1xs.at[part, p], r1xr.at[part, k], sr1x, part * 7 + k, d) for k, (p, d) in enumerate(xy_peers)
+        ])
+    sums = []
+    for part in range(2):
+        for c in copies_x[part]:
+            c.wait_recv()
+        fold(r1xs.at[part], xy, r1xr.at[part], r2fx, part * 8 * PX, SX, PX)
+        rows(r2xs, part, 8 * PX)[...] = rows(r2fx, part, 8 * PX)[...].astype(BF16)
+        sums.append([
+            send(rows(r2xs, part * 8 + p, PX), r2xr.at[part, k], sr2x, part * 7 + k, d)
+            for k, (p, d) in enumerate(z_peers)
+        ])
+        for c in copies_z[part]:
+            c.wait_recv()
+        fold(r1zs.at[part], z, r1zr.at[part], r2fz, part * 8 * PZ, SZ, PZ)
+        rows(r2zs, part, 8 * PZ)[...] = rows(r2fz, part, 8 * PZ)[...].astype(BF16)
+        sums[part] += [
+            send(rows(r2zs, part * 8 + p, PZ), r2zr.at[part, k], sr2z, part * 7 + k, d)
+            for k, (p, d) in enumerate(xy_peers)
+        ]
+        pending += copies_x[part] + copies_z[part] + sums[part]
+
+    squares = jnp.zeros((1, 1), F32)
+    logits = [jnp.zeros((1, 1), F32)] * 4
+    halves = []
+    for part in range(2):
+        for c in sums[part]:
+            c.wait_recv()
+        part_z = rows(r2fz, part * 8 + xy, PZ)[...]
+        part_x = rows(r2fx, part * 8 + z, PX)[...]
+        for k in range(7):
+            part_z = part_z + r2zr[part, k].astype(F32)
+            part_x = part_x + r2xr[part, k].astype(F32)
+        for c in range(2):
+            mine_rows = slice(c * 32 + part * 16, c * 32 + part * 16 + 16)
+            piece = jnp.concatenate(
+                [part_z[c * SZ // 2 : (c + 1) * SZ // 2], part_x[c * SX // 2 : (c + 1) * SX // 2]], axis=0
+            )
+            piece = hid[mine_rows] + piece
+            hid[mine_rows] = piece
+            gained = (piece * gain[mine_rows].astype(F32)).astype(BF16)
+            g1s[part * 32 + c * 16 : part * 32 + c * 16 + 16] = gained
+        halves.append([
+            send(rows(g1s, part * 2 + p % 2, 16), rows(g1r, part * 16 + zc, 16), sg1, part * 15 + k, d)
+            for k, (p, d) in enumerate(zc_peers)
+        ])
+        rows(g1r, part * 16 + zc, 16)[...] = rows(g1s, part * 2 + core, 16)[...]
+        for c in range(2):
+            mine_rows = slice(c * 32 + part * 16, c * 32 + part * 16 + 16)
+            piece = hid[mine_rows]
+            squares = squares + jnp.sum(piece * piece, keepdims=True)
+            gained = g1s[part * 32 + c * 16 : part * 32 + c * 16 + 16].astype(F32)
+            for e in range(4):
+                weight = router[e * 64 + c * 32 + part * 16 : e * 64 + c * 32 + part * 16 + 16]
+                logits[e] = logits[e] + jnp.sum(gained * weight, keepdims=True)
+    spread = lax.rsqrt(squares * (1.0 / 8192) + 1e-05)
+    logits = [v * spread for v in logits]
+
     first, second = ids_ref[0, 0], ids_ref[0, 1]
     zero = jnp.zeros((1, 1), F32)
     logit_a, logit_b = zero, zero
@@ -263,22 +286,14 @@
     gate_a = 1.0 / (1.0 + jnp.exp(logit_b - logit_a))
     gate_b = 1.0 / (1.0 + jnp.exp(logit_a - logit_b))
     lane = iota((8, 128), 1)
-    gates[...] = jnp.where(lane == first, gate_a, 0.0) + jnp.where(lane == second, gate_b, 0.0)
-    g1s[...] = normed
-
-    halves = [
-        [
-            send(rows(g1s, p % 2 * 2 + part, 16), rows(g1r, part * 16 + zc, 16), sg1, part * 15 + k, d)
-            for k, (p, d) in enumerate(zc_peers)
-        ]
-        for part in range(2)
-    ]
+    gates[...] = (
+        jnp.where(lane == first, gate_a, 0.0) + jnp.where(lane == second, gate_b, 0.0)
+        + jnp.where(lane == 4, spread, 0.0)
+    )
     gate_copies = [
         send(gates.at[pl.ds(0, 1)], gate_in.at[zc, pl.ds(0, 1)], sgate, k, d)
         for k, (p, d) in enumerate(zc_peers)
     ]
-    for part in range(2):
-        rows(g1r, part * 16 + zc, 16)[...] = rows(g1s, core * 2 + part, 16)[...]
     gate_in[zc] = gates[...]
     pending += halves[0] + halves[1] + gate_copies
 
@@ -294,7 +309,7 @@
 
     first_axis = [[d for _, d in y_peers], [d for _, d in x_peers]]
     second_axis = [[d for _, d in x_peers], [d for _, d in y_peers]]
-    across = []
+    across = [[], []]
     middle = [{}, {}]
     onward = [{}, {}]
 
@@ -304,7 +319,8 @@
             onward[part][k + j] = send(ref, ref, sg3, part * 12 + k + j, second_axis[part][to])
         if j == 2:
             onward[part][10] = send(ref, ref, sg3, part * 12 + 10, second_axis[part][1])
-        across.append(send(ref, ref, sg4, part * 10 + j, sibling))
+        if j == 2:
+            across[part].append(send(line(part, 0), line(part, 0), sg4, part * 10, sibling))
 
     def relay(part, j):
         if j % 2 == 0:
@@ -315,79 +331,91 @@
             ref, to = block(part, j, 3), second_axis[part][2]
         onward[part][8 + j] = send(ref, ref, sg3, part * 12 + 8 + j, to)
 
-    for part in range(2):
+    def begin(part):
         for c in halves[part]:
             c.wait_recv()
         g1f[...] = rows(g1r, part, 256)[...].astype(F32)
+        ref = block(part, 0, 0)
         for j in range(16):
-            block(part, 0, 0)[:, j * 128 : j * 128 + 128] = g1f[pl.ds(j, 16, stride=16), :].astype(BF16)
-        ref = block(part, 0, 0)
+            ref[:, j * 128 : j * 128 + 128] = g1f[pl.ds(j, 16, stride=16), :].astype(BF16)
         for k in (1, 0, 2):
             middle[part][k] = send(ref, ref, sg2, part * 3 + k, first_axis[part][k])
         pass_on(part, 0)
+
+    def come(part, j):
+        middle[part][j - 1].wait_recv()
+        pass_on(part, j)
+
+    def lines(part):
+        for j in (1, 2, 3):
+            onward[part][j].wait_recv()
+        across[part].append(send(line(part, 1), line(part, 1), sg4, part * 10 + 4, sibling))
+        for j in (0, 2):
+            onward[part][4 + j].wait_recv()
+        across[part].append(send(line(part, 3), line(part, 3), sg4, part * 10 + 5, sibling))
+
+    def last_line(part):
+        for j in (0, 1, 3, 2):
+            onward[part][8 + j].wait_recv()
+        across[part].append(send(line(part, 2), line(part, 2), sg4, part * 10 + 6, sibling))
+
+    begin(0)
+    begin(1)
     for j in (1, 3):
         for part in range(2):
-            middle[part][j - 1].wait_recv()
-            pass_on(part, j)
+            come(part, j)
     for part in range(2):
         relay(part, 0)
     for part in range(2):
-        middle[part][1].wait_recv()
-        pass_on(part, 2)
+        come(part, 2)
     for j in (1, 3):
         for part in range(2):
             relay(part, j)
+    lines(0)
+    lines(1)
     for c in gate_copies:
         c.wait_recv()
     for i in range(16):
         gate_all[y, x, i : i + 1] = gate_in[i, 0:1]
     ref = gate_all.at[y, x]
     gate_middle = [send(ref, ref, sgate, 15 + k, d) for k, d in enumerate(first_axis[0])]
-    for part in range(2):
-        for j in (1, 2, 3):
-            onward[part][j].wait_recv()
-        across.append(send(line(part, 1), line(part, 1), sg4, part * 10 + 4, sibling))
-        for j in (0, 2):
-            onward[part][4 + j].wait_recv()
-        across.append(send(line(part, 3), line(part, 3), sg4, part * 10 + 5, sibling))
+    last_line(0)
+    last_line(1)
     for c in gate_middle:
         c.wait_recv()
     ref = gate_all.at[:, x]
     gate_onward = [send(ref, ref, sgate, 18 + k, d) for k, d in enumerate(second_axis[0])]
-    for part in range(2):
-        for j in (0, 1, 3, 2):
-            onward[part][8 + j].wait_recv()
-            across.append(send(block(part, j, 2), block(part, j, 2), sg4, part * 10 + 6 + j, sibling))
-    pending += across + gate_middle + gate_onward
+    loads[2].wait()
+    loads[3].wait()
+    acc[...] = jnp.zeros_like(acc)
+
+    def into(half, part):
+        rows_in = (xa, xb)[part][half].reshape(256, 2048)
+        column = pl.ds(pl.multiple_of(half * 4096 + part * 2048, 2048), 2048)
+        for k in range(2):
+            acc[k] += nt(rows_in, w_in[k, :, column])
+
+    into(core, 0)
+    into(core, 1)
+    for c in across[0]:
+        c.wait_recv()
+    into(1 - core, 0)
+    for c in across[1]:
+        c.wait_recv()
+    into(1 - core, 1)
+    pending += across[0] + across[1] + gate_middle + gate_onward
     for part in range(2):
         pending += list(middle[part].values()) + list(onward[part].values())
 
-    for load in loads[2:5]:
-        load.wait()
-    acc[...] = jnp.zeros_like(acc)
-
-    def into(half):
-        def tile(t, _):
-            at = pl.multiple_of(t * TN, TN)
-            for part, ref in ((0, xa), (1, xb)):
-                rows_in = ref[half, :, :, :, pl.ds(at, TN)].reshape(256, TN)
-                column = pl.ds(pl.multiple_of(half * 4096 + part * 2048 + at, TN), TN)
-                acc[0] += nt(rows_in, w_in[0, :, column])
-                acc[1] += nt(rows_in, w_in[1, :, column])
-            return 0
-
-        lax.fori_loop(0, 2048 // TN, tile, 0)
-
-    into(core)
-    for c in across:
-        c.wait_recv()
-    into(1 - core)
-    gate_part = acc[0]
-    act[...] = (gate_part / (1.0 + jnp.exp(-gate_part)) * acc[1]).astype(BF16)
+    loads[4].wait()
     for c in gate_onward:
         c.wait_recv()
-    mine = iota((256, 128), 1) == tier
-    gate = jnp.sum(jnp.where(mine, gate_all[...].reshape(256, 128), 0.0), axis=1, keepdims=True)
+    row_facts = gate_all[...].reshape(256, 128)
+    lane = iota((256, 128), 1)
+    gate = jnp.sum(jnp.where(lane == tier, row_facts, 0.0), axis=1, keepdims=True)
+    factor = jnp.sum(jnp.where(lane == 4, row_facts, 0.0), axis=1, keepdims=True)
+    gate_part = acc[0] * factor
+    act[...] = (gate_part / (1.0 + jnp.exp(-gate_part)) * (acc[1] * factor)).astype(BF16)
 
     def down(half, part, t):
         column = pl.ds(pl.multiple_of(half * 4096 + part * 2048 + t * TN, TN), TN)
@@ -399,7 +427,8 @@
         return slice(t * TN, t * TN + TN)
 
     over = {}
-    for t in chunks:
+
+    def sibling_chunk(t):
         for part in range(2):
             f0s[part, :, :, :, cut(t)] = down(1 - core, part, t).astype(BF16).reshape(4, 4, 16, TN)
             at = (part, slice(None), slice(None), slice(None), cut(t))
@@ -480,12 +509,16 @@
                 last[half, k] = send(rows(f3s, half * 16 + p, 16), f3r.at[half, zc], sf3, half * 15 + k, d)
             f3r[half, zc] = rows(f3s, half * 16 + zc, 16)[...]
 
+    sibling_chunk(0)
+    sibling_chunk(1)
     own_chunk(0)
+    sibling_chunk(2)
     own_chunk(1)
+    sibling_chunk(3)
+    own_chunk(2)
     join_chunk(0)
-    own_chunk(2)
+    own_chunk(3)
     join_chunk(1)
-    own_chunk(3)
     join_chunk(2)
     end_chunk(0)
     end_chunk(1)
@@ -497,6 +530,8 @@
     finish_chunk(3)
     for sent in (over, plain, opposite, joined, final, last):
         pending += list(sent.values())
+    for c in pending:
+        c.wait_send()
     for c in last.values():
         c.wait_recv()
     sums = []
@@ -509,8 +544,6 @@
             parts.append(total)
         sums += [parts[0][:8], parts[1][:8], parts[0][8:], parts[1][8:]]
     out_ref[...] = (hid[...] + jnp.concatenate(sums, axis=0)).astype(BF16)
-    for c in pending:
-        c.wait_send()
 
 
 def on_device(
@@ -535,10 +568,9 @@
             v((1, 8192), BF16), v((64, 128), BF16), v((4, 8192), BF16),
             v((128, 128), BF16), v((128, 128), BF16), v((128, 128), F32), v((128, 128), BF16), v((128, 128), BF16),
             v((64, 128), F32), v((64, 128), F32), v((64, 128), F32), v((64, 128), F32),
-            v((8, 16, CZ // 2), BF16), v((7, 16, CZ // 2), BF16),
-            v((8, 16, CX // 2), BF16), v((7, 16, CX // 2), BF16),
-            v((8 * PZ, 128), BF16), v((7, PZ, 128), BF16), v((8 * PX, 128), BF16), v((7, PX, 128), BF16),
-            v((8 * PZ, 128), F32), v((8 * PX, 128), F32), v((64, 128), F32), v((256, 128), F32),
+            v((2, 8, 16, WZ), BF16), v((2, 7, 16, WZ), BF16), v((2, 8, 16, WX), BF16), v((2, 7, 16, WX), BF16),
+            v((16 * PZ, 128), BF16), v((2, 7, PZ, 128), BF16), v((16 * PX, 128), BF16), v((2, 7, PX, 128), BF16),
+            v((16 * PZ, 128), F32), v((16 * PX, 128), F32), v((64, 128), F32), v((256, 128), F32),
             v((64, 128), BF16), v((512, 128), BF16), v((256, 128), F32),
             v((8, 128), F32), v((16, 8, 128), F32), v((4, 4, 16, 128), F32),
             v((2, 4, 4, 16, 2048), BF16), v((2, 4, 4, 16, 2048), BF16),
@@ -547,7 +579,7 @@
             v((2, 4, 16, 2048), BF16), v((2, 4, 16, 2048), BF16), v((2, 4, 16, 2048), BF16), v((2, 4, 16, 2048), BF16),
             v((2, 4, 16, 2048), BF16), v((2, 3, 16, 2048), BF16),
             v((512, 128), F32), v((512, 128), BF16), v((2, 16, 16, 128), BF16),
-            sem(7), sem(7), sem(7), sem(7), sem(7), sem(7), sem(7), sem(7),
+            sem(7), sem(7), sem(7), sem(7), sem(14), sem(14), sem(14), sem(14),
             sem(30), sem(21), sem(6), sem(24), sem(20), sem(8), sem(24), sem(24), sem(30),
         ],
         compiler_params=pltpu.CompilerParams(

time: 104 us -> 100 us (0.962)
  Pallas kernels: 102 us -> 97.9 us
    pallas_call x1, Pallas kernels: 102 us -> 97.9 us  [on_device(): pl.pallas_call(kernel, out_shape=jax.ShapeDtypeStruct((64, 128), BF16), i...]
where the time goes in v4:
time: 100 us; the launch traced here: 99.9 us
  Pallas kernels  97.9 us (98%)
  local copies, waits for them, and re-layouts  1.36 us (1%)
    pallas_call x1, Pallas kernels, on_device(): pl.pallas_call(kernel, out_shape=jax.ShapeDtypeStruct((64, 128), BF16), i...  97.9 us

profile of v4, /device:TPU:1, one launch (start us, length us, event | category | flops | bytes accessed | tf_op | source)
XLA Modules:
  0.0 99.9 jit_solution(7040434372063473558)
XLA Ops:
  0.7 97.9 %shard_map.127 = bf16[64,128]{1,0:T(8,128)(2,1)} custom-call(s32[1,64]{1,0:T(1,128)} %home_ref.1, s32[1]{0:T(128)S(6)} %copy.17.len_ref, s32[1,2]{1,0:T(1,128)} %ids_ref.1, bf16[64,128]{1,0:T(8,128)(2,1)} %query_ref.1, bf16[32,64]{1,0:T(8,128)(2,1)} %bitcast.11, bf16[1,8192]{1,0:T(2,128)(2,1)} %resid_hbm.1, bf16[64,128]{1,0:T(8,128)(2,1)} %bitcast.10, ...), custom_call_target="tpu_custom_call" | custom-call | tf_op jit(solution)/shard_map/pallas_call | solution.py:560
  98.5 1.4 %copy.16 = bf16[1,1,64,128]{3,1,2,0:T(2,128)(2,1)} copy(bf16[1,1,64,128]{3,2,1,0:T(8,128)(2,1)} %bitcast.9) | data formatting | bytes 32768

commit v5 on v4

--- a/solution.py
+++ b/solution.py
@@ -387,15 +387,15 @@
     gate_onward = [send(ref, ref, sgate, 18 + k, d) for k, d in enumerate(second_axis[0])]
     loads[2].wait()
     loads[3].wait()
-    acc[...] = jnp.zeros_like(acc)
-
-    def into(half, part):
+
+    def into(half, part, first=False):
         rows_in = (xa, xb)[part][half].reshape(256, 2048)
         column = pl.ds(pl.multiple_of(half * 4096 + part * 2048, 2048), 2048)
         for k in range(2):
-            acc[k] += nt(rows_in, w_in[k, :, column])
-
-    into(core, 0)
+            product = nt(rows_in, w_in[k, :, column])
+            acc[k] = product if first else acc[k] + product
+
+    into(core, 0, first=True)
     into(core, 1)
     for c in across[0]:
         c.wait_recv()
@@ -570,7 +570,7 @@
             v((64, 128), F32), v((64, 128), F32), v((64, 128), F32), v((64, 128), F32),
             v((2, 8, 16, WZ), BF16), v((2, 7, 16, WZ), BF16), v((2, 8, 16, WX), BF16), v((2, 7, 16, WX), BF16),
             v((16 * PZ, 128), BF16), v((2, 7, PZ, 128), BF16), v((16 * PX, 128), BF16), v((2, 7, PX, 128), BF16),
-            v((16 * PZ, 128), F32), v((16 * PX, 128), F32), v((64, 128), F32), v((256, 128), F32),
+            v((16 * PZ, 128), F32), v((16 * PX, 128), F32), v((64, 128), F32), v((512, 128), F32),
             v((64, 128), BF16), v((512, 128), BF16), v((256, 128), F32),
             v((8, 128), F32), v((16, 8, 128), F32), v((4, 4, 16, 128), F32),
             v((2, 4, 4, 16, 2048), BF16), v((2, 4, 4, 16, 2048), BF16),

time: 100 us -> 100 us (level)
  no operation moved by 1% of the time
where the time goes in v5:
time: 100 us; the launch traced here: 99.9 us
  Pallas kernels  97.9 us (98%)
  local copies, waits for them, and re-layouts  1.36 us (1%)
    pallas_call x1, Pallas kernels, on_device(): pl.pallas_call(kernel, out_shape=jax.ShapeDtypeStruct((64, 128), BF16), i...  97.9 us

profile of v5, /device:TPU:1, one launch (start us, length us, event | category | flops | bytes accessed | tf_op | source)
XLA Modules:
  0.0 99.9 jit_solution(9762232023164954896)
XLA Ops:
  0.7 97.9 %shard_map.127 = bf16[64,128]{1,0:T(8,128)(2,1)} custom-call(s32[1,64]{1,0:T(1,128)} %home_ref.1, s32[1]{0:T(128)S(6)} %copy.17.len_ref, s32[1,2]{1,0:T(1,128)} %ids_ref.1, bf16[64,128]{1,0:T(8,128)(2,1)} %query_ref.1, bf16[32,64]{1,0:T(8,128)(2,1)} %bitcast.11, bf16[1,8192]{1,0:T(2,128)(2,1)} %resid_hbm.1, bf16[64,128]{1,0:T(8,128)(2,1)} %bitcast.10, ...), custom_call_target="tpu_custom_call" | custom-call | tf_op jit(solution)/shard_map/pallas_call | solution.py:560
  98.5 1.4 %copy.16 = bf16[1,1,64,128]{3,1,2,0:T(2,128)(2,1)} copy(bf16[1,1,64,128]{3,2,1,0:T(8,128)(2,1)} %bitcast.9) | data formatting | bytes 32768

commit v6 on v5

--- a/solution.py
+++ b/solution.py
@@ -400,6 +400,12 @@
     for c in across[0]:
         c.wait_recv()
     into(1 - core, 0)
+    for c in gate_onward:
+        c.wait_recv()
+    row_facts = gate_all[...].reshape(256, 128)
+    lane = iota((256, 128), 1)
+    gate = jnp.sum(jnp.where(lane == tier, row_facts, 0.0), axis=1, keepdims=True)
+    factor = jnp.sum(jnp.where(lane == 4, row_facts, 0.0), axis=1, keepdims=True)
     for c in across[1]:
         c.wait_recv()
     into(1 - core, 1)
@@ -408,12 +414,6 @@
         pending += list(middle[part].values()) + list(onward[part].values())
 
     loads[4].wait()
-    for c in gate_onward:
-        c.wait_recv()
-    row_facts = gate_all[...].reshape(256, 128)
-    lane = iota((256, 128), 1)
-    gate = jnp.sum(jnp.where(lane == tier, row_facts, 0.0), axis=1, keepdims=True)
-    factor = jnp.sum(jnp.where(lane == 4, row_facts, 0.0), axis=1, keepdims=True)
     gate_part = acc[0] * factor
     act[...] = (gate_part / (1.0 + jnp.exp(-gate_part)) * (acc[1] * factor)).astype(BF16)
 

time: 100 us -> 101 us (1.010)
  no operation moved by 1% of the time
where the time goes in v6:
time: 101 us
  Pallas kernels  98.7 us (98%)
  local copies, waits for them, and re-layouts  1.36 us (1%)
    pallas_call x1, Pallas kernels, on_device(): pl.pallas_call(kernel, out_shape=jax.ShapeDtypeStruct((64, 128), BF16), i...  98.7 us

profile of v6, /device:TPU:1, one launch (start us, length us, event | category | flops | bytes accessed | tf_op | source)
XLA Modules:
  0.0 100.7 jit_solution(16064693407648080035)
XLA Ops:
  0.7 98.7 %shard_map.127 = bf16[64,128]{1,0:T(8,128)(2,1)} custom-call(s32[1,64]{1,0:T(1,128)} %home_ref.1, s32[1]{0:T(128)S(6)} %copy.17.len_ref, s32[1,2]{1,0:T(1,128)} %ids_ref.1, bf16[64,128]{1,0:T(8,128)(2,1)} %query_ref.1, bf16[32,64]{1,0:T(8,128)(2,1)} %bitcast.11, bf16[1,8192]{1,0:T(2,128)(2,1)} %resid_hbm.1, bf16[64,128]{1,0:T(8,128)(2,1)} %bitcast.10, ...), custom_call_target="tpu_custom_call" | custom-call | tf_op jit(solution)/shard_map/pallas_call | solution.py:560
  99.3 1.4 %copy.16 = bf16[1,1,64,128]{3,1,2,0:T(2,128)(2,1)} copy(bf16[1,1,64,128]{3,2,1,0:T(8,128)(2,1)} %bitcast.9) | data formatting | bytes 32768
